TPU v7x, 32 devices: a whole 2x2x4 slice. The times are simulated.
32 devices in a mesh: groups: 2 (over y), rep: 4 (over z), tp: 4 (over x, core).
Axes of the slice: x: 2, y: 2, z: 4, core: 2. Of those that a mesh axis runs over, the one named last changes fastest.
Arguments:
- hidden: bfloat16 [1024, 8192], P(('groups', 'rep'), 'tp'), parts along dimension 0, may hold values from -6 to 6
- queries: bfloat16 [1024, 8192], P(('groups', 'rep'), 'tp'), parts along dimension 0, may hold values from -5 to 5
- fresh_token_keys: bfloat16 [1024, 1024], P(('groups', 'rep'), 'tp'), parts along dimension 0, may hold values from -5 to 5
- cached_key_rows: bfloat16 [1024, 32, 1024], P(('groups', 'rep'), None, 'tp'), parts along dimension 0, may hold values from -5 to 5
- cached_value_rows: bfloat16 [1024, 32, 1024], P(('groups', 'rep'), None, 'tp'), parts along dimension 0, may hold values from -6 to 6
- lengths: int32 [1024], P(('groups', 'rep')), parts along dimension 0, may hold values from 1 to 32, as said below
- row_adapter_index: int32 [1024], P(('groups', 'rep')), parts along dimension 0, may hold values from 0 to 127, as said below
- adapter_table_place: int32 [256], P('groups'), parts along dimension 0, may hold values from 0 to 127, as said below
- value_projection_matrix: bfloat16 [8192, 1024], P(None, 'tp'), may hold values from -0.0625 to 0.0625
- adapter_down_factor: bfloat16 [256, 16, 8192], P(('groups', 'rep'), None, 'tp'), parts along dimension 0, may hold values from -0.0625 to 0.0625
- adapter_up_factor: bfloat16 [256, 16, 1024], P(('groups', 'rep'), None, 'tp'), parts along dimension 0, may hold values from -1.5 to 1.5
Outputs:
- value_new: bfloat16 [1024, 1024], P(('groups', 'rep'), 'tp'), parts along dimension 0
- attended: bfloat16 [1024, 8192], P(('groups', 'rep'), 'tp'), parts along dimension 0
There are 2 independent parts, one for each index of `groups`. A program takes and returns all parts, laid end to end along the dimension named above; an argument that names none is the same for every part. Nothing has to cross between parts.
Inputs may be any that keep to these rules, and one draw needn't show every extreme that they name: `row_adapter_index`: at most 64 of the 128 rows of one index of rep use adapters a whose adapter_table_place[a] // 32 is one and the same index of rep; some index of rep receives exactly 64 such rows from every index of rep. `adapter_table_place`: A permutation of the adapters. `lengths`: some row holds 32 live positions.
All inputs are finite; a program needn't handle non-finite values.
Results may differ from a plain program's by a relative error of at most 0.01.
Values may be sent and summed in bfloat16 or wider, within the bound.
A program may use at most 64 MiB of HBM per device.

v0:
```python
import jax
import jax.numpy as jnp
from jax import lax
from jax.sharding import PartitionSpec as P

HD = 128


adapter_scale = 2.0


def shards(
    hidden,
    queries,
    fresh_token_keys,
    cached_key_rows,
    cached_value_rows,
    lengths,
    row_adapter_index,
    adapter_table_place,
    value_projection_matrix,
    adapter_down_factor,
    adapter_up_factor,
):
    replicas = lax.axis_size("rep")
    row_count = hidden.shape[0]
    stored_tables = adapter_down_factor.shape[0]
    local_value_output = adapter_up_factor.shape[2]
    capacity = max(2, (2 * row_count + replicas - 1) // replicas)
    slot_total = replicas * capacity
    base = jnp.dot(
        lax.all_gather(hidden, "tp", axis=1, tiled=True),
        value_projection_matrix,
        preferred_element_type=jnp.float32,
    )
    table_places = jnp.take(adapter_table_place, row_adapter_index)
    owner = table_places // stored_tables
    inner = table_places % stored_tables
    owner_hot = (owner[:, None] == jnp.arange(replicas, dtype=jnp.int32)[None, :]).astype(jnp.int32)
    before = jnp.cumsum(owner_hot, axis=0) - owner_hot
    position = jnp.sum(before * owner_hot, axis=1)
    slot_pos = owner * capacity + position
    dispatch = slot_pos[None, :] == jnp.arange(slot_total, dtype=jnp.int32)[:, None]
    inner_buf = jnp.sum(jnp.where(dispatch, inner[None, :], 0), axis=1)
    wanted = lax.all_to_all(inner_buf, "rep", split_axis=0, concat_axis=0, tiled=True)
    pick = (wanted[:, None] == jnp.arange(stored_tables, dtype=jnp.int32)[None, :]).astype(
        jnp.bfloat16
    )
    flattened_up_factor = adapter_up_factor.reshape(stored_tables, -1)
    up_sel = jnp.dot(pick, flattened_up_factor, preferred_element_type=jnp.float32).astype(
        jnp.bfloat16
    )
    outgoing = jnp.dot(
        dispatch.astype(jnp.bfloat16), hidden, preferred_element_type=jnp.float32
    ).astype(jnp.bfloat16)
    gathered_factors = lax.all_to_all(outgoing, "rep", split_axis=0, concat_axis=0, tiled=True)
    complete_set = jnp.einsum(
        "jf,ypf->jyp", gathered_factors, adapter_down_factor, preferred_element_type=jnp.float32
    )
    partial_sum = jnp.einsum("sak,sa->sk", complete_set, pick.astype(jnp.float32))
    reduced_input = lax.psum(partial_sum, "tp").astype(jnp.bfloat16)
    up_factor_places = up_sel.reshape(slot_total, -1, local_value_output)
    slot_delta = (
        adapter_scale
        * jnp.einsum(
            "qj,qjw->qw", reduced_input, up_factor_places, preferred_element_type=jnp.float32
        )
    ).astype(jnp.bfloat16)
    returned = lax.all_to_all(slot_delta, "rep", split_axis=0, concat_axis=0, tiled=True)
    adapter_update = jnp.take(returned, slot_pos, axis=0)
    value_new = (base + adapter_update.astype(jnp.float32)).astype(jnp.bfloat16)
    kv_local = fresh_token_keys.shape[1] // HD
    group_size = queries.shape[1] // fresh_token_keys.shape[1]
    positions = cached_key_rows.shape[1]
    inverse = 1.0 / HD**0.5
    query_heads = queries.reshape(row_count, kv_local, group_size, HD)
    key_heads = cached_key_rows.reshape(row_count, positions, kv_local, HD)
    value_heads = cached_value_rows.reshape(row_count, positions, kv_local, HD)
    scores = (
        jnp.einsum("rghd,rcgd->rghc", query_heads, key_heads, preferred_element_type=jnp.float32)
        * inverse
    )
    own = (
        jnp.einsum(
            "rghd,rgd->rgh",
            query_heads,
            fresh_token_keys.reshape(row_count, kv_local, HD),
            preferred_element_type=jnp.float32,
        )
        * inverse
    )
    live = (jnp.arange(positions, dtype=jnp.int32)[None, :] < lengths[:, None])[:, None, None, :]
    top = jnp.maximum(jnp.max(jnp.where(live, scores, -jnp.inf), axis=-1), own)
    expo = jnp.where(live, jnp.exp(scores - top[..., None]), 0.0)
    own_expo = jnp.exp(own - top)
    total = jnp.sum(expo, axis=-1) + own_expo
    weights = (expo / total[..., None]).astype(jnp.bfloat16)
    own_weight = (own_expo / total).astype(jnp.bfloat16)
    mixed = jnp.einsum("rghc,rcgd->rghd", weights, value_heads, preferred_element_type=jnp.float32)
    mixed = mixed + own_weight.astype(jnp.float32)[..., None] * value_new.astype(
        jnp.float32
    ).reshape(row_count, kv_local, 1, HD)
    attended = mixed.reshape(row_count, -1).astype(jnp.bfloat16)
    return (value_new, attended)


def solution(mesh):
    return jax.shard_map(
        shards,
        mesh=mesh,
        in_specs=(
            P(("groups", "rep"), "tp"),
            P(("groups", "rep"), "tp"),
            P(("groups", "rep"), "tp"),
            P(("groups", "rep"), None, "tp"),
            P(("groups", "rep"), None, "tp"),
            P(("groups", "rep")),
            P(("groups", "rep")),
            P("groups"),
            P(None, "tp"),
            P(("groups", "rep"), None, "tp"),
            P(("groups", "rep"), None, "tp"),
        ),
        out_specs=(P(("groups", "rep"), "tp"), P(("groups", "rep"), "tp")),
        check_vma=False,
    )
```

profile of v0, /device:TPU:0, one launch (start us, length us, event | category | flops | bytes accessed | tf_op | source)
XLA Modules:
  0.0 99.0 jit_solution(16761915026765819655)
XLA Ops:
  7.2 0.8 compare_select_fusion.1
  8.0 1.6 %gather_fusion = s32[128]{0:T(128)S(1)} fusion(s32[128]{0:T(128)} %param.18, s32[1024]{0:T(1024)S(1)} %pad_clamp_fusion.1), kind=kCustom, calls=%fused_computation | custom fusion | bytes 1536 | tf_op jit(solution)/shard_map/jit(_take)/gather | solution.py:36
  12.0 6.3 %all-to-all-start.1 = ((s32[4,64,1]{1,2,0:T(1,128)}), s32[4,64,1]{1,2,0:T(1,128)S(1)}, u32[]{:S(2)}, u32[]{:S(2)}) async-start(s32[4,64,1]{1,2,0:T(1,128)} %bitcast.3), calls=%async_computation.1 | async-start | bytes 4096 | tf_op jit(solution)/shard_map/all_to_all | solution.py:45
  19.0 2.4 %convolution_convert_fusion.1 = bf16[256,2048]{1,0:T(8,128)(2,1)} fusion(bf16[128,2048]{1,0:T(8,128)(2,1)} %param.11, s32[128]{0:T(128)S(1)} %get-tuple-element.3), kind=kOutput, calls=%fused_computation.3 | convolution fusion | flops 134774784 | bytes 1573376 | tf_op jit(solution)/shard_map/dot_general | solution.py:53
  21.6 0.9 copy.52
  22.5 1.3 %all-to-all-done.1 = s32[4,64,1]{1,2,0:T(1,128)S(1)} async-done(((s32[4,64,1]{1,2,0:T(1,128)}), s32[4,64,1]{1,2,0:T(1,128)S(1)}, u32[]{:S(2)}, u32[]{:S(2)}) %all-to-all-start.1) | async-done | bytes 1056 | tf_op jit(solution)/shard_map/all_to_all | solution.py:45
  23.8 4.2 %all-to-all-start = ((bf16[4,64,2048]{2,1,0:T(8,128)(2,1)}), bf16[4,64,2048]{2,1,0:T(8,128)(2,1)}, u32[]{:S(2)}, u32[]{:S(2)}) async-start(bf16[4,64,2048]{2,1,0:T(8,128)(2,1)} %bitcast), calls=%async_computation | async-start | bytes 2097152 | tf_op jit(solution)/shard_map/all_to_all | solution.py:56
  28.1 3.3 %select_reduce_fusion = (f32[128,2,8]{2,1,0:T(2,128)S(1)}, f32[128,2,8,32]{3,2,1,0:T(8,128)S(1)}) fusion(pred[128,32]{1,0:T(8,128)(4,1)S(1)} %iota_compare_fusion.4, bf16[128,2,8,128]{3,2,1,0:T(8,128)(2,1)} %bitcast.82, bf16[128,32,256]{2,1,0:T(8,128)(2,1)} %param.14), kind=kOutput, calls=%fused_computation.19 | convolution fusion | flops 16971776 | bytes 2895872 | tf_op jit(solution)/shard_map/rghd,rcgd->rghc/dot_general | solution.py:80
  32.2 0.9 reshape.160
  33.0 2.1 %fusion.36 = f32[128,2,1,8]{3,2,1,0:T(1,128)} fusion(bf16[128,2,8,128]{3,2,1,0:T(8,128)(2,1)} %bitcast.83, bf16[128,2,128,1]{2,3,1,0:T(2,128)(2,1)S(1)} %reshape.160), kind=kOutput, calls=%fused_computation.62 | convolution fusion | flops 524288 | bytes 598016 | tf_op jit(solution)/shard_map/rghd,rgd->rgh/dot_general | solution.py:84
  35.1 1.0 copy.47
  36.7 1.3 %fusion.32 = f32[128,2,8]{0,2,1:T(8,128)} fusion(f32[128,2,8]{0,2,1:T(8,128)} %copy.35, f32[128,2,1,8]{0,3,1,2:T(8,128)S(1)} %copy.47), kind=kLoop, calls=%fused_computation.46 | loop fusion | flops 4096 | bytes 24576 | tf_op jit(solution)/shard_map/max | solution.py:93
  38.0 0.8 copy.36
  38.9 1.5 %fusion.18 = f32[128,2,8]{2,1,0:T(2,128)} fusion(f32[128,2,8,32]{3,2,1,0:T(8,128)S(1)} %get-tuple-element.9, f32[128,2,8]{2,1,0:T(2,128)S(1)} %copy.36, pred[128,32]{1,0:T(8,128)(4,1)S(1)} %iota_compare_fusion.4), kind=kLoop, calls=%fused_computation.20 | loop fusion | flops 194560 | bytes 282624 | tf_op jit(solution)/shard_map/reduce_sum | solution.py:96
  40.3 1.6 %copy.37 = f32[128,2,8]{0,2,1:T(8,128)} copy(f32[128,2,8]{2,1,0:T(2,128)} %fusion.18) | data formatting | bytes 16384 | tf_op jit(solution)/shard_map/reduce_sum | solution.py:96
  41.9 1.3 %fusion.34 = (f32[128,2,8]{0,2,1:T(8,128)}, f32[128,2,8]{0,2,1:T(8,128)}) fusion(f32[128,2,8]{0,2,1:T(8,128)} %copy.37, f32[128,2,1,8]{0,3,1,2:T(8,128)} %copy-done.4, f32[128,2,8]{0,2,1:T(8,128)} %copy.35), kind=kLoop, calls=%fused_computation.52 | loop fusion | flops 14336 | bytes 40960 | tf_op jit(solution)/shard_map/add | solution.py:96
  43.7 1.9 %reduce.3 = s32[4,64]{1,0:T(4,128)} reduce(s32[4,64,1]{1,2,0:T(1,128)} %copy-done.8, s32[]{:T(128)} %broadcast.126), dimensions={2}, to_apply=%all_to_all.26.reduce_sub_computation.3 | reduce | bytes 2052 | tf_op jit(solution)/shard_map/all_to_all | solution.py:45
  45.7 1.3 %eq.49 = s32[256]{0:T(256)} reshape(s32[4,64]{1,0:T(4,128)} %reduce.3) | data formatting | bytes 2048 | tf_op jit(solution)/shard_map/eq | solution.py:46
  47.0 1.4 %convolution_convert_fusion = bf16[256,4096]{1,0:T(8,128)(2,1)S(1)} fusion(bf16[32,4096]{1,0:T(8,128)(2,1)S(1)} %bitcast.84, s32[256]{0:T(256)} %eq.49), kind=kOutput, calls=%fused_computation.2 | convolution fusion | flops 68165632 | bytes 2360320 | tf_op jit(solution)/shard_map/dot_general | solution.py:50
  48.4 2.0 %copy.51 = bf16[32,8,16,256]{3,2,1,0:T(8,128)(2,1)} copy(bf16[32,8,16,256]{3,1,2,0:T(8,128)(2,1)S(1)} %bitcast.80) | data formatting | bytes 4194304
  51.1 1.8 %all-to-all-done = bf16[4,64,2048]{2,1,0:T(8,128)(2,1)} async-done(((bf16[4,64,2048]{2,1,0:T(8,128)(2,1)}), bf16[4,64,2048]{2,1,0:T(8,128)(2,1)}, u32[]{:S(2)}, u32[]{:S(2)}) %all-to-all-start) | async-done | bytes 1048608 | tf_op jit(solution)/shard_map/all_to_all | solution.py:56
  52.9 3.5 %fusion.6 = bf16[256,32,16]{0,1,2:T(8,128)(2,1)S(1)} fusion(bf16[256,2048,1]{1,0,2:T(8,128)(2,1)} %bitcast.2, bf16[32,16,2048]{2,1,0:T(8,128)(2,1)} %param.20), kind=kOutput, calls=%fused_computation.10 | convolution fusion | flops 536870912 | bytes 3407872 | tf_op jit(solution)/shard_map/jf,ypf->jyp/dot_general | solution.py:57
  56.4 1.9 %copy.41 = bf16[256,32,16]{1,2,0:T(8,128)(2,1)} copy(bf16[256,32,16]{0,1,2:T(8,128)(2,1)S(1)} %fusion.6) | data formatting | bytes 524288 | tf_op jit(solution)/shard_map/jf,ypf->jyp/dot_general | solution.py:57
  58.3 1.9 %fusion.22 = f32[256,1,16]{2,1,0:T(1,128)S(1)} fusion(bf16[256,32,16]{1,2,0:T(8,128)(2,1)} %copy.41, pred[256,32,1]{1,0,2:T(32,128)(4,1)} %fusion.28), kind=kOutput, calls=%fused_computation.25 | convolution fusion | flops 262144 | bytes 286720 | tf_op jit(solution)/shard_map/sak,sa->sk/dot_general | solution.py:60
  60.2 11.6 %psum.7 = bf16[256,16]{1,0:T(8,128)(2,1)S(1)} all-reduce(f32[256,16]{1,0:T(8,128)S(1)} %bitcast.90), channel_id=1, replica_groups=mesh['groups'=2,'rep'=4,'tp'=4] {'tp'}, use_global_device_ids=true, to_apply=%region_3.4 | all-reduce | flops 4096 | bytes 24576 | tf_op jit(solution)/shard_map/psum | solution.py:61
  71.8 2.0 %fusion.26 = f32[256,1,256]{2,1,0:T(1,128)S(1)} fusion(bf16[256,16,256]{2,1,0:T(8,128)(2,1)} %bitcast.79, bf16[256,16,1]{1,0,2:T(8,128)(2,1)S(1)} %bitcast.85), kind=kOutput, calls=%fused_computation.30 | convolution fusion | flops 2097152 | bytes 2367488 | tf_op jit(solution)/shard_map/qj,qjw->qw/dot_general | solution.py:65
  74.5 3.3 %all-to-all-start.2 = ((bf16[4,64,256]{2,1,0:T(8,128)(2,1)}), bf16[4,64,256]{2,1,0:T(8,128)(2,1)S(1)}, u32[]{:S(2)}, u32[]{:S(2)}) async-start(bf16[4,64,256]{2,1,0:T(8,128)(2,1)} %bitcast.9), calls=%async_computation.2 | async-start | bytes 262144 | tf_op jit(solution)/shard_map/all_to_all | solution.py:69
  79.4 4.8 %all-to-all-done.2 = bf16[4,64,256]{2,1,0:T(8,128)(2,1)S(1)} async-done(((bf16[4,64,256]{2,1,0:T(8,128)(2,1)}), bf16[4,64,256]{2,1,0:T(8,128)(2,1)S(1)}, u32[]{:S(2)}, u32[]{:S(2)}) %all-to-all-start.2) | async-done | bytes 131104 | tf_op jit(solution)/shard_map/all_to_all | solution.py:69
  84.2 0.8 gather_fusion.1
  85.1 3.5 %fusion.17 = bf16[128,256]{1,0:T(8,128)(2,1)S(1)} fusion(bf16[128,8192]{1,0:T(8,128)(2,1)} %all-gather.2.cloned.1.call-done, bf16[8192,256]{1,0:T(8,128)(2,1)} %param.19, bf16[128,256]{1,0:T(8,128)(2,1)S(1)} %gather_fusion.1, pred[128]{0:T(512)(128)(4,1)S(1)} %copy-done.11), kind=kOutput, calls=%fused_computation.16 | convolution fusion | flops 537001984 | bytes 6422656 | tf_op jit(solution)/shard_map/dot_general | solution.py:31
  88.7 2.5 %fusion.14 = bf16[128,2,8,128]{3,2,1,0:T(8,128)(2,1)S(1)} fusion(f32[128,2,8,32]{3,2,1,0:T(8,128)S(1)} %get-tuple-element.9, f32[128,2,128]{2,1,0:T(2,128)S(1)} %reshape.133, f32[128,2,8]{2,1,0:T(2,128)} %copy.40, f32[128,2,8]{2,1,0:T(2,128)} %copy.38, f32[128,2,8]{2,1,0:T(2,128)S(1)} %copy.36, pred[128,32]{1,0:T(8,128)(4,1)S(1)} %iota_compare_fusion.4, ...), kind=kOutput, calls=%fused_computation.14 | convolution fusion | flops 17825792 | bytes 3043328 | tf_op jit(solution)/shard_map/rghc,rcgd->rghd/dot_general | solution.py:99
  91.3 0.9 copy.78
  (49 shorter events, 8.2 us)
Async XLA Ops:
  7.2 81.6 %copy-start = (bf16[128,32,256]{2,1,0:T(8,128)(2,1)S(1)}, bf16[128,32,256]{2,1,0:T(8,128)(2,1)}, u32[]{:S(2)}) copy-start(bf16[128,32,256]{2,1,0:T(8,128)(2,1)} %param.15) | copy-start | bytes 6291460
  7.2 14.3 %copy-start.12 = (s32[128]{0:T(128)S(1)}, s32[128]{0:T(128)}, u32[]{:S(2)}) copy-start(s32[128]{0:T(128)} %param.16) | copy-start | bytes 1540
  7.2 14.4 %copy-start.1 = (bf16[128,2048]{1,0:T(8,128)(2,1)S(1)}, bf16[128,2048]{1,0:T(8,128)(2,1)}, u32[]{:S(2)}) copy-start(bf16[128,2048]{1,0:T(8,128)(2,1)} %param.12) | copy-start | bytes 1572868
  11.2 12.6 %copy-start.9 = (s32[128]{0:T(128)}, s32[128]{0:T(128)S(1)}, u32[]{:S(2)}) copy-start(s32[128]{0:T(128)S(1)} %get-tuple-element.3) | copy-start | bytes 1540
  12.0 11.8 %all-to-all-start.1 = ((s32[4,64,1]{1,2,0:T(1,128)}), s32[4,64,1]{1,2,0:T(1,128)S(1)}, u32[]{:S(2)}, u32[]{:S(2)}) async-start(s32[4,64,1]{1,2,0:T(1,128)} %bitcast.3), calls=%async_computation.1 | async-start | bytes 4096 | tf_op jit(solution)/shard_map/all_to_all | solution.py:45
  18.3 66.8 %all-gather.2.cloned.1.call-start = ((), (), s32[]{:S(2)}) async-start(), calls=%async_computation.3 | async-start | bytes 2621440 | tf_op jit(solution)/shard_map/all_gather | solution.py:32
  23.8 4.3 %copy-start.8 = (s32[4,64,1]{1,2,0:T(1,128)}, s32[4,64,1]{1,2,0:T(1,128)S(1)}, u32[]{:S(2)}) copy-start(s32[4,64,1]{1,2,0:T(1,128)S(1)} %all-to-all-done.1) | copy-start | bytes 3076
  23.8 29.1 %all-to-all-start = ((bf16[4,64,2048]{2,1,0:T(8,128)(2,1)}), bf16[4,64,2048]{2,1,0:T(8,128)(2,1)}, u32[]{:S(2)}, u32[]{:S(2)}) async-start(bf16[4,64,2048]{2,1,0:T(8,128)(2,1)} %bitcast), calls=%async_computation | async-start | bytes 2097152 | tf_op jit(solution)/shard_map/all_to_all | solution.py:56
  28.1 3.3 %copy-start.3 = (bf16[32,16,256]{2,1,0:T(8,128)(2,1)S(1)}, bf16[32,16,256]{2,1,0:T(8,128)(2,1)}, u32[]{:S(2)}) copy-start(bf16[32,16,256]{2,1,0:T(8,128)(2,1)} %param.21) | copy-start | bytes 786436
  36.1 0.6 copy-start.4
  48.4 2.0 %copy-start.7 = (s32[256]{0:T(256)S(1)}, s32[256]{0:T(256)}, u32[]{:S(2)}) copy-start(s32[256]{0:T(256)} %eq.49) | copy-start | bytes 3076
  60.1 17.7 %copy-start.10 = (s32[128]{0:T(128)S(1)}, s32[128]{0:T(128)}, u32[]{:S(2)}) copy-start(s32[128]{0:T(128)} %copy-done.9) | copy-start | bytes 1540
  60.1 17.7 %copy-start.6 = (f32[128,2,8]{0,2,1:T(8,128)S(1)}, f32[128,2,8]{0,2,1:T(8,128)}, u32[]{:S(2)}) copy-start(f32[128,2,8]{0,2,1:T(8,128)} %get-tuple-element.6) | copy-start | bytes 24580
  60.2 18.5 %copy-start.5 = (f32[128,2,8]{0,2,1:T(8,128)S(1)}, f32[128,2,8]{0,2,1:T(8,128)}, u32[]{:S(2)}) copy-start(f32[128,2,8]{0,2,1:T(8,128)} %get-tuple-element.7) | copy-start | bytes 24580
  60.2 24.9 %copy-start.11 = (pred[128]{0:T(512)(128)(4,1)S(1)}, pred[128]{0:T(512)(128)(4,1)}, u32[]{:S(2)}) copy-start(pred[128]{0:T(512)(128)(4,1)} %get-tuple-element.2) | copy-start | bytes 388
  74.5 9.7 %all-to-all-start.2 = ((bf16[4,64,256]{2,1,0:T(8,128)(2,1)}), bf16[4,64,256]{2,1,0:T(8,128)(2,1)S(1)}, u32[]{:S(2)}, u32[]{:S(2)}) async-start(bf16[4,64,256]{2,1,0:T(8,128)(2,1)} %bitcast.9), calls=%async_computation.2 | async-start | bytes 262144 | tf_op jit(solution)/shard_map/all_to_all | solution.py:69
  88.6 2.6 %copy-start.2 = (bf16[128,256]{1,0:T(8,128)(2,1)}, bf16[128,256]{1,0:T(8,128)(2,1)S(1)}, u32[]{:S(2)}) copy-start(bf16[128,256]{1,0:T(8,128)(2,1)S(1)} %fusion.17) | copy-start | bytes 196612
Sparse Core Ops, SparseCore 0:
  20.7 24.0 all-gather.1
where the time goes:
time: 100 us; the launch traced here: 99 us
  matrix products  22.7 us (23%)
  local copies, waits for them, and re-layouts  17.8 us (18%)
  between operations  14.3 us (14%)
  starting transfers between devices  13.9 us (14%)
  blocking collectives  11.6 us (12%)
  other arithmetic  10.1 us (10%)
  waiting for transfers between devices  8.6 us (9%)
    psum x1, blocking collectives, shards(): reduced_input = lax.psum(partial_sum, 'tp').astype(jnp.bfloat16)  11.6 us
    all_to_all x1, starting transfers between devices, shards(): lax.all_to_all(inner_buf, 'rep', split_axis=0, concat_axis=0, tiled=True)  6.32 us
    all_to_all x1, waiting for transfers between devices, shards(): lax.all_to_all(slot_delta, 'rep', split_axis=0, concat_axis=0, tiled=True)  4.78 us
    unnamed x30, local copies, waits for them, and re-layouts  4.54 us
    all_to_all x1, starting transfers between devices, shards(): lax.all_to_all(outgoing, 'rep', split_axis=0, concat_axis=0, tiled=True)  4.24 us
    dot_general x1, matrix products, shards(): jnp.dot(lax.all_gather(hidden, 'tp', axis=1, tiled=True), value_projectio...  3.54 us
    dot_general x1, matrix products, shards(): jnp.einsum('jf,ypf->jyp', gathered_factors, adapter_down_factor, preferre...  3.51 us
    all_to_all x1, starting transfers between devices, shards(): lax.all_to_all(slot_delta, 'rep', split_axis=0, concat_axis=0, tiled=True)  3.33 us
  transfers between devices with their start and end apart: 4, of which 3 were waited for; matrix products, arithmetic and copies ran while one was open for 39% of the time, Pallas kernels for 0%

commit v1 on v0

v1 whole, which is shorter than its diff:
```python
import functools

import jax
import jax.numpy as jnp
from jax import lax
from jax.experimental import pallas as pl
from jax.experimental.pallas import tpu as pltpu
from jax.sharding import PartitionSpec as P

HD = 128
ROW_BLOCK = 16
ADAPTER_SCALE = 2.0
MASKED = -1e30
F32, BF16 = jnp.float32, jnp.bfloat16
NT = (((1,), (1,)), ((), ()))
TN = (((0,), (0,)), ((), ()))
NN = (((1,), (0,)), ((), ()))


def dot(a, b, dims=NN):
    return lax.dot_general(a, b, dims, preferred_element_type=F32)


def iota(shape, dim):
    return lax.broadcasted_iota(jnp.int32, shape, dim)


def kernel(
    reps, tps, cap, stored, rank,
    hidden, fresh, lengths, index, places, q_hbm, k_hbm, v_hbm, w_hbm, down_hbm, up_hbm,
    value_out, attended_out,
    q_v, k_v, v_v, w_v, down_v, up_v, local_sem,
    shards, out_rows, in_rows, out_ids, in_ids, slots, part, parts, out_delta, in_delta,
    mixed_v, own_v, length_v, value_v, attended_v,
    gather_send, gather_recv, row_send, row_recv, id_send, id_recv,
    part_send, part_recv, delta_send, delta_recv,
):
    me_r, me_t = lax.axis_index("rep"), lax.axis_index("tp")
    rows, kv_local = hidden.shape[0], fresh.shape[1] // HD
    group = q_v.shape[1] // fresh.shape[1]
    positions = k_v.shape[1]
    span = ROW_BLOCK * positions

    def rep_at(k):
        return lax.rem(me_r + k, reps)

    def tp_at(k):
        return lax.rem(me_t + k, tps)

    sibling = me_t + 1 - 2 * lax.rem(me_t, 2)

    barrier = pltpu.get_barrier_semaphore()

    def greet_rep(k, c):
        pl.semaphore_signal(barrier, inc=1, device_id={"rep": rep_at(k)}, device_id_type=pl.DeviceIdType.MESH)
        return c

    def greet_tp(k, c):
        pl.semaphore_signal(barrier, inc=1, device_id={"tp": tp_at(k)}, device_id_type=pl.DeviceIdType.MESH)
        return c

    lax.fori_loop(1, reps, greet_rep, 0)
    lax.fori_loop(1, tps, greet_tp, 0)

    loads = [
        pltpu.make_async_copy(src, dst, local_sem.at[n])
        for n, (src, dst) in enumerate(
            ((q_hbm, q_v), (k_hbm, k_v), (v_hbm, v_v), (down_hbm, down_v), (w_hbm, w_v), (up_hbm, up_v))
        )
    ]
    for load in loads:
        load.start()

    adapters = places.shape[1]
    place = places[...].astype(F32)
    owner_tab = jnp.floor((place + 0.5) / stored)
    inner_tab = place - owner_tab * stored
    hot = (iota((adapters, rows), 0) == index[...]).astype(F32).astype(BF16)
    owner = dot(jnp.broadcast_to(owner_tab, (8, adapters)).astype(BF16), hot)
    inner = dot(jnp.broadcast_to(inner_tab, (8, adapters)).astype(BF16), hot).astype(BF16)
    rep_pad = max(8, reps)
    owner_row = owner[0:1, :]
    owner_hot = (iota((rep_pad, rows), 0).astype(F32) == owner_row).astype(F32)
    earlier = (iota((rows, rows), 0) < iota((rows, rows), 1)).astype(F32).astype(BF16)
    before = dot(owner_hot.astype(BF16), earlier)
    position = jnp.sum(before * owner_hot, axis=0, keepdims=True)
    slot_iota = iota((rows, rows), 0).astype(F32)

    def gather_copy(src, to, q, n):
        return pltpu.make_async_remote_copy(
            src_ref=src, dst_ref=shards.at[q], send_sem=gather_send.at[n], recv_sem=gather_recv.at[q],
            device_id={"tp": to}, device_id_type=pl.DeviceIdType.MESH,
        )

    def row_copy(d):
        return pltpu.make_async_remote_copy(
            src_ref=out_rows.at[d], dst_ref=in_rows.at[me_r], send_sem=row_send.at[d], recv_sem=row_recv.at[me_r],
            device_id={"rep": d}, device_id_type=pl.DeviceIdType.MESH,
        )

    def id_copy(d):
        return pltpu.make_async_remote_copy(
            src_ref=out_ids.at[d], dst_ref=in_ids.at[me_r], send_sem=id_send.at[d], recv_sem=id_recv.at[me_r],
            device_id={"rep": d}, device_id_type=pl.DeviceIdType.MESH,
        )

    def row_arrival(s):
        return pltpu.make_async_remote_copy(
            src_ref=out_rows.at[s], dst_ref=in_rows.at[s], send_sem=row_send.at[s], recv_sem=row_recv.at[s],
            device_id={"rep": s}, device_id_type=pl.DeviceIdType.MESH,
        )

    def id_arrival(s):
        return pltpu.make_async_remote_copy(
            src_ref=out_ids.at[s], dst_ref=in_ids.at[s], send_sem=id_send.at[s], recv_sem=id_recv.at[s],
            device_id={"rep": s}, device_id_type=pl.DeviceIdType.MESH,
        )

    def fill(d):
        member = jnp.where(owner_row == d.astype(F32), position, -1.0)
        dispatch = (slot_iota == member).astype(F32).astype(BF16)
        slots[d] = dispatch
        return dispatch

    pl.semaphore_wait(barrier, reps - 1 + tps - 1)

    def send_rows(i, c):
        d = rep_at(1 + lax.rem(i + (reps - 1) // 2, reps - 1))
        dispatch = fill(d)
        out_rows[d] = dot(dispatch[:cap], hidden[...]).astype(BF16)
        row_copy(d).start()
        out_ids[d] = dot(inner, dispatch, NT)
        id_copy(d).start()
        return c

    lax.fori_loop(0, reps - 1, send_rows, 0)

    half = tps // 2
    gather_copy(hidden, sibling, me_t, 0).start()
    for k in range(1, half):
        gather_copy(hidden, tp_at(2 * k), me_t, k).start()

    dispatch = fill(me_r)
    in_rows[me_r] = dot(dispatch[:cap], hidden[...]).astype(BF16)
    in_ids[me_r] = dot(inner, dispatch, NT)

    diagonal = iota((rows, rows), 0) == iota((rows, rows), 1)
    length_col = jnp.sum(jnp.where(diagonal, lengths[...].astype(F32), 0.0), axis=1, keepdims=True)
    length_v[...] = jnp.broadcast_to(length_col, (rows, HD))

    inverse = 1.0 / HD**0.5
    loads[0].wait()
    loads[1].wait()
    loads[2].wait()

    def attend(b, c):
        at = pl.ds(pl.multiple_of(b * ROW_BLOCK, ROW_BLOCK), ROW_BLOCK)
        column = iota((ROW_BLOCK, span), 1).astype(F32)
        low = (iota((ROW_BLOCK, span), 0) * positions).astype(F32)
        high = low + length_v[at, 0:1]
        bias = jnp.where((column >= low) & (column < high), 0.0, MASKED)
        for g in range(kv_local):
            feats = slice(g * HD, (g + 1) * HD)
            heads = [slice((g * group + j) * HD, (g * group + j + 1) * HD) for j in range(group)]
            query = jnp.concatenate([q_v[at, h] for h in heads], axis=0)
            keys = k_v[at, :, feats].reshape(span, HD)
            values = v_v[at, :, feats].reshape(span, HD)
            scores = dot(query, keys, NT).reshape(group, ROW_BLOCK, span) * inverse + bias[None]
            own = (
                jnp.sum(
                    query.astype(F32).reshape(group, ROW_BLOCK, HD) * fresh[at, feats].astype(F32)[None],
                    axis=-1, keepdims=True,
                )
                * inverse
            )
            top = jnp.maximum(jnp.max(scores, axis=-1, keepdims=True), own)
            expo = jnp.exp(scores - top)
            own_expo = jnp.exp(own - top)
            scale = 1.0 / (jnp.sum(expo, axis=-1, keepdims=True) + own_expo)
            weights = (expo * scale).astype(BF16).reshape(group * ROW_BLOCK, span)
            own_weight = jnp.broadcast_to(
                (own_expo * scale).astype(BF16).astype(F32), (group, ROW_BLOCK, HD)
            )
            mixed = dot(weights, values)
            for j, h in enumerate(heads):
                mixed_v[at, h] = mixed[j * ROW_BLOCK:(j + 1) * ROW_BLOCK]
                own_v[at, h] = own_weight[j]
        return c

    blocks = rows // ROW_BLOCK
    early = blocks // 2
    lax.fori_loop(0, early, attend, 0)
    for k in range(1, half):
        q = tp_at(2 * k)
        gather_copy(hidden, q, q, 0).wait_recv()
        gather_copy(shards.at[q], sibling, q, half + k).start()
    lax.fori_loop(early, blocks, attend, 0)

    loads[4].wait()
    base = dot(hidden[...], w_v[me_t])
    for k in range(1, half):
        q = tp_at(2 * k)
        base = base + dot(shards[q], w_v[q])
    for k in range(half):
        q = lax.rem(sibling + 2 * k, tps)
        gather_copy(hidden, q, q, 0).wait_recv()
        base = base + dot(shards[q], w_v[q])

    loads[3].wait()
    loads[5].wait()

    def part_copy(k, s):
        return pltpu.make_async_remote_copy(
            src_ref=part.at[s], dst_ref=parts.at[me_t, s], send_sem=part_send.at[k, s],
            recv_sem=part_recv.at[me_t, s], device_id={"tp": tp_at(k)}, device_id_type=pl.DeviceIdType.MESH,
        )

    def part_arrival(k, s):
        q = tp_at(k)
        return pltpu.make_async_remote_copy(
            src_ref=part.at[s], dst_ref=parts.at[q, s], send_sem=part_send.at[k, s],
            recv_sem=part_recv.at[q, s], device_id={"tp": q}, device_id_type=pl.DeviceIdType.MESH,
        )

    def delta_copy(s):
        return pltpu.make_async_remote_copy(
            src_ref=out_delta.at[s], dst_ref=in_delta.at[me_r], send_sem=delta_send.at[s],
            recv_sem=delta_recv.at[me_r], device_id={"rep": s}, device_id_type=pl.DeviceIdType.MESH,
        )

    def delta_arrival(s):
        return pltpu.make_async_remote_copy(
            src_ref=out_delta.at[s], dst_ref=in_delta.at[s], send_sem=delta_send.at[s],
            recv_sem=delta_recv.at[s], device_id={"rep": s}, device_id_type=pl.DeviceIdType.MESH,
        )

    def chosen(s):
        return iota((stored, rank, cap), 0).astype(F32) == in_ids[s][0:1, :cap].reshape(1, 1, cap)

    def shrink(s):
        full = dot(down_v[...], in_rows[s], NT).reshape(stored, rank, cap)
        part[s] = jnp.sum(jnp.where(chosen(s), full, 0.0), axis=0)
        for k in range(1, tps):
            part_copy(k, s).start()

    def expand(s):
        total = part[s]
        for k in range(1, tps):
            part_arrival(k, s).wait_recv()
            total = total + parts[tp_at(k), s]
        total = total.astype(BF16).astype(F32)
        spread = jnp.where(chosen(s), total[None], 0.0).reshape(stored * rank, cap).astype(BF16)
        return (ADAPTER_SCALE * dot(spread, up_v[...], TN)).astype(BF16)

    def step(i, c):
        s = rep_at(i)
        row_arrival(s).wait_recv()
        id_arrival(s).wait_recv()
        shrink(s)

        @pl.when(i == 1)
        def _():
            in_delta[me_r] = expand(me_r)

        @pl.when(i > 1)
        def _():
            back = rep_at(i - 1)
            out_delta[back] = expand(back)
            delta_copy(back).start()

        return c

    shrink(me_r)
    lax.fori_loop(1, reps, step, 0)
    last = rep_at(reps - 1)
    out_delta[last] = expand(last)
    delta_copy(last).start()

    value_v[...] = base + dot(slots[me_r][:cap], in_delta[me_r], TN)

    def collect(i, c):
        s = rep_at(reps - i)
        delta_arrival(s).wait_recv()
        value_v[...] += dot(slots[s][:cap], in_delta[s], TN)
        return c

    lax.fori_loop(1, reps, collect, 0)

    value = value_v[...].astype(BF16)
    value_out[...] = value
    fresh_value = value.astype(F32)
    for g in range(kv_local):
        for j in range(group):
            h = slice((g * group + j) * HD, (g * group + j + 1) * HD)
            attended_out[:, h] = (mixed_v[:, h] + own_v[:, h] * fresh_value[:, g * HD:(g + 1) * HD]).astype(BF16)

    gather_copy(hidden, sibling, me_t, 0).wait_send()
    for k in range(1, half):
        gather_copy(hidden, sibling, me_t, k).wait_send()
        gather_copy(hidden, sibling, me_t, half + k).wait_send()

    def drain(i, c):
        d = rep_at(i)
        row_copy(d).wait_send()
        id_copy(d).wait_send()
        delta_copy(d).wait_send()
        return c

    lax.fori_loop(1, reps, drain, 0)

    def drain_parts(s, c):
        for k in range(1, tps):
            part_copy(k, s).wait_send()
        return c

    lax.fori_loop(0, reps, drain_parts, 0)


def shards_fn(
    hidden, queries, fresh_token_keys, cached_key_rows, cached_value_rows, lengths, row_adapter_index,
    adapter_table_place, value_projection_matrix, adapter_down_factor, adapter_up_factor,
):
    reps, tps = lax.axis_size("rep"), lax.axis_size("tp")
    rows, width = hidden.shape
    stored, rank, _ = adapter_down_factor.shape
    out_width = adapter_up_factor.shape[2]
    cap = max(2, (2 * rows + reps - 1) // reps)
    dma = pltpu.SemaphoreType.DMA
    vmem = pltpu.VMEM
    w = value_projection_matrix.reshape(tps, width, out_width)
    scratch = [
        vmem(queries.shape, BF16), vmem(cached_key_rows.shape, BF16), vmem(cached_value_rows.shape, BF16),
        vmem(w.shape, BF16), vmem((stored * rank, width), BF16), vmem((stored * rank, out_width), BF16), dma((6,)),
        vmem((tps, rows, width), BF16),
        vmem((reps, cap, width), BF16), vmem((reps, cap, width), BF16),
        vmem((reps, 8, rows), F32), vmem((reps, 8, rows), F32),
        vmem((reps, rows, rows), BF16),
        vmem((reps, rank, cap), F32), vmem((tps, reps, rank, cap), F32),
        vmem((reps, cap, out_width), BF16), vmem((reps, cap, out_width), BF16),
        vmem(queries.shape, F32), vmem(queries.shape, F32), vmem((rows, HD), F32), vmem((rows, out_width), F32),
        vmem((8, 128), F32),
        dma((tps,)), dma((tps,)), dma((reps,)), dma((reps,)), dma((reps,)), dma((reps,)),
        dma((tps, reps)), dma((tps, reps)), dma((reps,)), dma((reps,)),
    ]
    vm, anywhere = pl.BlockSpec(memory_space=pltpu.VMEM), pl.BlockSpec(memory_space=pl.ANY)
    return pl.pallas_call(
        functools.partial(kernel, reps, tps, cap, stored, rank),
        out_shape=(
            jax.ShapeDtypeStruct((rows, out_width), BF16),
            jax.ShapeDtypeStruct(queries.shape, BF16),
        ),
        in_specs=[vm] * 5 + [anywhere] * 6,
        out_specs=(vm, vm),
        scratch_shapes=scratch,
        compiler_params=pltpu.CompilerParams(
            collective_id=0, has_side_effects=True, vmem_limit_bytes=48 * 1024 * 1024
        ),
    )(
        hidden, fresh_token_keys, lengths.reshape(1, rows), row_adapter_index.reshape(1, rows),
        adapter_table_place.reshape(1, -1), queries, cached_key_rows, cached_value_rows, w,
        adapter_down_factor.reshape(stored * rank, width), adapter_up_factor.reshape(stored * rank, out_width),
    )


def solution(mesh):
    return jax.shard_map(
        shards_fn,
        mesh=mesh,
        in_specs=(
            P(("groups", "rep"), "tp"),
            P(("groups", "rep"), "tp"),
            P(("groups", "rep"), "tp"),
            P(("groups", "rep"), None, "tp"),
            P(("groups", "rep"), None, "tp"),
            P(("groups", "rep")),
            P(("groups", "rep")),
            P("groups"),
            P(None, "tp"),
            P(("groups", "rep"), None, "tp"),
            P(("groups", "rep"), None, "tp"),
        ),
        out_specs=(P(("groups", "rep"), "tp"), P(("groups", "rep"), "tp")),
        check_vma=False,
    )
```

time: 100 us -> 51.7 us (0.52)
  Pallas kernels: 0 us -> 40.2 us
  matrix products: 22.7 us -> 0 us
  starting transfers between devices: 13.9 us -> 0 us
  between operations: 14.3 us -> 0.66 us
  blocking collectives: 11.6 us -> 0 us
  other arithmetic: 10.1 us -> 0 us
  waiting for transfers between devices: 8.6 us -> 0 us
  local copies, waits for them, and re-layouts: 17.8 us -> 10.4 us
    pallas_call x0 -> x1, Pallas kernels: none -> 40.2 us  [shards_fn(): pl.pallas_call(functools.partial(kernel, reps, tps, cap, stored, rank), o...]
    dot_general x9 -> x0, matrix products: 22.7 us -> none  [the longest x1 3.54 us: shards(): jnp.dot(lax.all_gather(hidden, 'tp', axis=1, tiled=True), value_projectio...]
    all_to_all x3 -> x0, starting transfers between devices: 13.9 us -> none  [the longest x1 6.32 us: shards(): lax.all_to_all(inner_buf, 'rep', split_axis=0, concat_axis=0, tiled=True)]
    psum x1 -> x0, blocking collectives: 11.6 us -> none  [shards(): reduced_input = lax.psum(partial_sum, 'tp').astype(jnp.bfloat16)]
    all_to_all x3 -> x0, waiting for transfers between devices: 7.86 us -> none  [the longest x1 4.78 us: shards(): lax.all_to_all(slot_delta, 'rep', split_axis=0, concat_axis=0, tiled=True)]
    unnamed x30 -> x20, local copies, waits for them, and re-layouts: 4.54 us -> 10.4 us
    dot_general x2 -> x0, local copies, waits for them, and re-layouts: 2.81 us -> none  [the longest x1 1.86 us: shards(): jnp.einsum('jf,ypf->jyp', gathered_factors, adapter_down_factor, preferre...]
    gather x2 -> x0, local copies, waits for them, and re-layouts: 2.43 us -> none  [the longest x1 1.58 us: shards(): table_places = jnp.take(adapter_table_place, row_adapter_index)]
  transfers between devices with their start and end apart: 4 -> 0, of which waited for: 3 -> 0; matrix products, arithmetic and copies ran while one was open for 39% -> 0% of each run, Pallas kernels for 0% -> 0%
where the time goes in v1:
time: 51.7 us; the launch traced here: 51.3 us
  Pallas kernels  40.2 us (78%)
  local copies, waits for them, and re-layouts  10.4 us (20%)
  between operations  0.66 us (1%)
    pallas_call x1, Pallas kernels, shards_fn(): pl.pallas_call(functools.partial(kernel, reps, tps, cap, stored, rank), o...  40.2 us
    unnamed x20, local copies, waits for them, and re-layouts  10.4 us

profile of v1, /device:TPU:0, one launch (start us, length us, event | category | flops | bytes accessed | tf_op | source)
XLA Modules:
  0.0 51.3 jit_solution(15778474153140990717)
XLA Ops:
  0.6 0.0 copy-start
  0.6 1.6 %copy-done = bf16[128,32,256]{2,1,0:T(8,128)(2,1)S(1)} copy-done((bf16[128,32,256]{2,1,0:T(8,128)(2,1)S(1)}, bf16[128,32,256]{2,1,0:T(8,128)(2,1)}, u32[]{:S(2)}) %copy-start) | copy-done | bytes 2097176
  2.2 0.0 copy-start.1
  2.2 1.6 %copy-done.1 = bf16[128,32,256]{2,1,0:T(8,128)(2,1)S(1)} copy-done((bf16[128,32,256]{2,1,0:T(8,128)(2,1)S(1)}, bf16[128,32,256]{2,1,0:T(8,128)(2,1)}, u32[]{:S(2)}) %copy-start.1) | copy-done | bytes 2097176
  3.8 0.0 copy-start.2
  3.8 1.0 %copy-done.2 = bf16[128,2048]{1,0:T(8,128)(2,1)S(1)} copy-done((bf16[128,2048]{1,0:T(8,128)(2,1)S(1)}, bf16[128,2048]{1,0:T(8,128)(2,1)}, u32[]{:S(2)}) %copy-start.2) | copy-done | bytes 524312
  4.9 0.0 copy-start.3
  4.9 1.0 %copy-done.3 = bf16[128,2048]{1,0:T(8,128)(2,1)S(1)} copy-done((bf16[128,2048]{1,0:T(8,128)(2,1)S(1)}, bf16[128,2048]{1,0:T(8,128)(2,1)}, u32[]{:S(2)}) %copy-start.3) | copy-done | bytes 524312
  5.9 0.0 copy-start.4
  5.9 0.9 %copy-done.4 = bf16[32,16,256]{2,1,0:T(8,128)(2,1)S(1)} copy-done((bf16[32,16,256]{2,1,0:T(8,128)(2,1)S(1)}, bf16[32,16,256]{2,1,0:T(8,128)(2,1)}, u32[]{:S(2)}) %copy-start.4) | copy-done | bytes 262168
  6.9 0.0 copy-start.5
  6.9 0.8 %copy-done.5 = bf16[128,256]{1,0:T(8,128)(2,1)S(1)} copy-done((bf16[128,256]{1,0:T(8,128)(2,1)S(1)}, bf16[128,256]{1,0:T(8,128)(2,1)}, u32[]{:S(2)}) %copy-start.5) | copy-done | bytes 65560
  7.7 0.0 copy-start.6
  7.7 0.7 %copy-done.6 = s32[128]{0:T(128)S(1)} copy-done((s32[128]{0:T(128)S(1)}, s32[128]{0:T(128)}, u32[]{:S(2)}) %copy-start.6) | copy-done | bytes 536
  8.3 0.0 copy-start.7
  8.4 0.7 %copy-done.7 = s32[128]{0:T(128)S(1)} copy-done((s32[128]{0:T(128)S(1)}, s32[128]{0:T(128)}, u32[]{:S(2)}) %copy-start.7) | copy-done | bytes 536
  9.0 0.0 copy-start.8
  9.0 0.7 %copy-done.8 = s32[128]{0:T(128)S(1)} copy-done((s32[128]{0:T(128)S(1)}, s32[128]{0:T(128)}, u32[]{:S(2)}) %copy-start.8) | copy-done | bytes 536
  9.7 40.2 %shard_map.122 = (bf16[128,256]{1,0:T(8,128)(2,1)S(1)}, bf16[128,2048]{1,0:T(8,128)(2,1)S(1)}) custom-call(bf16[128,2048]{1,0:T(8,128)(2,1)S(1)} %copy-done.2, bf16[128,256]{1,0:T(8,128)(2,1)S(1)} %copy-done.5, s32[1,128]{1,0:T(1,128)S(1)} %bitcast.7, s32[1,128]{1,0:T(1,128)S(1)} %bitcast.8, s32[1,128]{1,0:T(1,128)S(1)} %bitcast.9, ...), custom_call_target="tpu_custom_call" | custom-call | tf_op jit(solution)/shard_map/pallas_call | solution.py:346
  49.9 0.6 %copy.15 = bf16[128,256]{1,0:T(8,128)(2,1)} copy(bf16[128,256]{1,0:T(8,128)(2,1)S(1)} %get-tuple-element.4) | data formatting | bytes 131072
  50.5 0.8 %copy.16 = bf16[128,2048]{1,0:T(8,128)(2,1)} copy(bf16[128,2048]{1,0:T(8,128)(2,1)S(1)} %get-tuple-element.5) | data formatting | bytes 1048576
Async XLA Ops:
  0.6 1.6 %copy-start = (bf16[128,32,256]{2,1,0:T(8,128)(2,1)S(1)}, bf16[128,32,256]{2,1,0:T(8,128)(2,1)}, u32[]{:S(2)}) copy-start(bf16[128,32,256]{2,1,0:T(8,128)(2,1)} %k_hbm.1) | copy-start | bytes 6291460
  2.2 1.6 %copy-start.1 = (bf16[128,32,256]{2,1,0:T(8,128)(2,1)S(1)}, bf16[128,32,256]{2,1,0:T(8,128)(2,1)}, u32[]{:S(2)}) copy-start(bf16[128,32,256]{2,1,0:T(8,128)(2,1)} %v_hbm.1) | copy-start | bytes 6291460
  3.8 1.0 %copy-start.2 = (bf16[128,2048]{1,0:T(8,128)(2,1)S(1)}, bf16[128,2048]{1,0:T(8,128)(2,1)}, u32[]{:S(2)}) copy-start(bf16[128,2048]{1,0:T(8,128)(2,1)} %hidden.1) | copy-start | bytes 1572868
  4.9 1.0 %copy-start.3 = (bf16[128,2048]{1,0:T(8,128)(2,1)S(1)}, bf16[128,2048]{1,0:T(8,128)(2,1)}, u32[]{:S(2)}) copy-start(bf16[128,2048]{1,0:T(8,128)(2,1)} %q_hbm.1) | copy-start | bytes 1572868
  5.9 0.9 %copy-start.4 = (bf16[32,16,256]{2,1,0:T(8,128)(2,1)S(1)}, bf16[32,16,256]{2,1,0:T(8,128)(2,1)}, u32[]{:S(2)}) copy-start(bf16[32,16,256]{2,1,0:T(8,128)(2,1)} %param.21) | copy-start | bytes 786436
  6.9 0.8 %copy-start.5 = (bf16[128,256]{1,0:T(8,128)(2,1)S(1)}, bf16[128,256]{1,0:T(8,128)(2,1)}, u32[]{:S(2)}) copy-start(bf16[128,256]{1,0:T(8,128)(2,1)} %fresh.1) | copy-start | bytes 196612
  7.7 0.7 %copy-start.6 = (s32[128]{0:T(128)S(1)}, s32[128]{0:T(128)}, u32[]{:S(2)}) copy-start(s32[128]{0:T(128)} %param.16) | copy-start | bytes 1540
  8.3 0.7 %copy-start.7 = (s32[128]{0:T(128)S(1)}, s32[128]{0:T(128)}, u32[]{:S(2)}) copy-start(s32[128]{0:T(128)} %param.17) | copy-start | bytes 1540
  9.0 0.7 %copy-start.8 = (s32[128]{0:T(128)S(1)}, s32[128]{0:T(128)}, u32[]{:S(2)}) copy-start(s32[128]{0:T(128)} %param.18) | copy-start | bytes 1540

commit v2 on v1

--- a/solution.py
+++ b/solution.py
@@ -27,11 +27,12 @@
 
 def kernel(
     reps, tps, cap, stored, rank,
-    hidden, fresh, lengths, index, places, q_hbm, k_hbm, v_hbm, w_hbm, down_hbm, up_hbm,
+    hidden_hbm, fresh_hbm, lengths_hbm, index_hbm, places_hbm, q_hbm, k_hbm, v_hbm, w_hbm, down_hbm, up_hbm,
     value_out, attended_out,
+    hidden, fresh, lengths, index, places,
     q_v, k_v, v_v, w_v, down_v, up_v, local_sem,
     shards, out_rows, in_rows, out_ids, in_ids, slots, part, parts, out_delta, in_delta,
-    mixed_v, own_v, length_v, value_v, attended_v,
+    mixed_v, own_v, length_v, value_v,
     gather_send, gather_recv, row_send, row_recv, id_send, id_recv,
     part_send, part_recv, delta_send, delta_recv,
 ):
@@ -44,33 +45,44 @@
     def rep_at(k):
         return lax.rem(me_r + k, reps)
 
+    rep_sibling = me_r + 1 - 2 * lax.rem(me_r, 2)
+
+    def rep_near(i):
+        odd = lax.rem(i, 2)
+        return lax.rem(odd * rep_sibling + (1 - odd) * me_r + 2 * (i // 2), reps)
+
     def tp_at(k):
         return lax.rem(me_t + k, tps)
 
     sibling = me_t + 1 - 2 * lax.rem(me_t, 2)
-
-    barrier = pltpu.get_barrier_semaphore()
-
-    def greet_rep(k, c):
-        pl.semaphore_signal(barrier, inc=1, device_id={"rep": rep_at(k)}, device_id_type=pl.DeviceIdType.MESH)
-        return c
-
-    def greet_tp(k, c):
-        pl.semaphore_signal(barrier, inc=1, device_id={"tp": tp_at(k)}, device_id_type=pl.DeviceIdType.MESH)
-        return c
-
-    lax.fori_loop(1, reps, greet_rep, 0)
-    lax.fori_loop(1, tps, greet_tp, 0)
 
     loads = [
         pltpu.make_async_copy(src, dst, local_sem.at[n])
         for n, (src, dst) in enumerate(
-            ((q_hbm, q_v), (k_hbm, k_v), (v_hbm, v_v), (down_hbm, down_v), (w_hbm, w_v), (up_hbm, up_v))
+            (
+                (q_hbm, q_v), (k_hbm, k_v), (v_hbm, v_v), (down_hbm, down_v), (w_hbm, w_v), (up_hbm, up_v),
+                (index_hbm, index), (places_hbm, places), (hidden_hbm, hidden), (lengths_hbm, lengths), (fresh_hbm, fresh),
+            )
         )
     ]
-    for load in loads:
-        load.start()
-
+    for n in (6, 7, 8, 9, 10, 0, 1, 2, 3, 5, 4):
+        loads[n].start()
+
+    barrier = pltpu.get_barrier_semaphore()
+
+    def greet_rep(k, c):
+        pl.semaphore_signal(barrier, inc=1, device_id={"rep": rep_at(k)}, device_id_type=pl.DeviceIdType.MESH)
+        return c
+
+    def greet_tp(k, c):
+        pl.semaphore_signal(barrier, inc=1, device_id={"tp": tp_at(k)}, device_id_type=pl.DeviceIdType.MESH)
+        return c
+
+    lax.fori_loop(1, reps, greet_rep, 0)
+    lax.fori_loop(1, tps, greet_tp, 0)
+
+    loads[6].wait()
+    loads[7].wait()
     adapters = places.shape[1]
     place = places[...].astype(F32)
     owner_tab = jnp.floor((place + 0.5) / stored)
@@ -122,10 +134,11 @@
         slots[d] = dispatch
         return dispatch
 
+    loads[8].wait()
     pl.semaphore_wait(barrier, reps - 1 + tps - 1)
 
     def send_rows(i, c):
-        d = rep_at(1 + lax.rem(i + (reps - 1) // 2, reps - 1))
+        d = rep_near(reps - 1 - i)
         dispatch = fill(d)
         out_rows[d] = dot(dispatch[:cap], hidden[...]).astype(BF16)
         row_copy(d).start()
@@ -144,6 +157,7 @@
     in_rows[me_r] = dot(dispatch[:cap], hidden[...]).astype(BF16)
     in_ids[me_r] = dot(inner, dispatch, NT)
 
+    loads[9].wait()
     diagonal = iota((rows, rows), 0) == iota((rows, rows), 1)
     length_col = jnp.sum(jnp.where(diagonal, lengths[...].astype(F32), 0.0), axis=1, keepdims=True)
     length_v[...] = jnp.broadcast_to(length_col, (rows, HD))
@@ -152,6 +166,7 @@
     loads[0].wait()
     loads[1].wait()
     loads[2].wait()
+    loads[10].wait()
 
     def attend(b, c):
         at = pl.ds(pl.multiple_of(b * ROW_BLOCK, ROW_BLOCK), ROW_BLOCK)
@@ -253,7 +268,7 @@
         return (ADAPTER_SCALE * dot(spread, up_v[...], TN)).astype(BF16)
 
     def step(i, c):
-        s = rep_at(i)
+        s = rep_near(i)
         row_arrival(s).wait_recv()
         id_arrival(s).wait_recv()
         shrink(s)
@@ -264,7 +279,7 @@
 
         @pl.when(i > 1)
         def _():
-            back = rep_at(i - 1)
+            back = rep_near(i - 1)
             out_delta[back] = expand(back)
             delta_copy(back).start()
 
@@ -272,14 +287,14 @@
 
     shrink(me_r)
     lax.fori_loop(1, reps, step, 0)
-    last = rep_at(reps - 1)
+    last = rep_near(reps - 1)
     out_delta[last] = expand(last)
     delta_copy(last).start()
 
     value_v[...] = base + dot(slots[me_r][:cap], in_delta[me_r], TN)
 
     def collect(i, c):
-        s = rep_at(reps - i)
+        s = rep_near(i)
         delta_arrival(s).wait_recv()
         value_v[...] += dot(slots[s][:cap], in_delta[s], TN)
         return c
@@ -328,9 +343,12 @@
     dma = pltpu.SemaphoreType.DMA
     vmem = pltpu.VMEM
     w = value_projection_matrix.reshape(tps, width, out_width)
+    adapters = adapter_table_place.shape[0]
     scratch = [
+        vmem(hidden.shape, BF16), vmem(fresh_token_keys.shape, BF16),
+        vmem((1, rows), jnp.int32), vmem((1, rows), jnp.int32), vmem((1, adapters), jnp.int32),
         vmem(queries.shape, BF16), vmem(cached_key_rows.shape, BF16), vmem(cached_value_rows.shape, BF16),
-        vmem(w.shape, BF16), vmem((stored * rank, width), BF16), vmem((stored * rank, out_width), BF16), dma((6,)),
+        vmem(w.shape, BF16), vmem((stored * rank, width), BF16), vmem((stored * rank, out_width), BF16), dma((11,)),
         vmem((tps, rows, width), BF16),
         vmem((reps, cap, width), BF16), vmem((reps, cap, width), BF16),
         vmem((reps, 8, rows), F32), vmem((reps, 8, rows), F32),
@@ -338,7 +356,6 @@
         vmem((reps, rank, cap), F32), vmem((tps, reps, rank, cap), F32),
         vmem((reps, cap, out_width), BF16), vmem((reps, cap, out_width), BF16),
         vmem(queries.shape, F32), vmem(queries.shape, F32), vmem((rows, HD), F32), vmem((rows, out_width), F32),
-        vmem((8, 128), F32),
         dma((tps,)), dma((tps,)), dma((reps,)), dma((reps,)), dma((reps,)), dma((reps,)),
         dma((tps, reps)), dma((tps, reps)), dma((reps,)), dma((reps,)),
     ]
@@ -349,11 +366,11 @@
             jax.ShapeDtypeStruct((rows, out_width), BF16),
             jax.ShapeDtypeStruct(queries.shape, BF16),
         ),
-        in_specs=[vm] * 5 + [anywhere] * 6,
+        in_specs=[anywhere] * 11,
         out_specs=(vm, vm),
         scratch_shapes=scratch,
         compiler_params=pltpu.CompilerParams(
-            collective_id=0, has_side_effects=True, vmem_limit_bytes=48 * 1024 * 1024
+            collective_id=0, has_side_effects=True, vmem_limit_bytes=60 * 1024 * 1024
         ),
     )(
         hidden, fresh_token_keys, lengths.reshape(1, rows), row_adapter_index.reshape(1, rows),

time: 51.7 us -> 44.5 us (0.86)
  local copies, waits for them, and re-layouts: 10.4 us -> 3.35 us
    unnamed x20 -> x2, local copies, waits for them, and re-layouts: 10.4 us -> 3.35 us
where the time goes in v2:
time: 44.5 us; the launch traced here: 44.3 us
  Pallas kernels  40.3 us (91%)
  local copies, waits for them, and re-layouts  3.35 us (8%)
  between operations  0.64 us (1%)
    pallas_call x1, Pallas kernels, shards_fn(): pl.pallas_call(functools.partial(kernel, reps, tps, cap, stored, rank), o...  40.3 us
    unnamed x2, local copies, waits for them, and re-layouts  3.35 us

profile of v2, /device:TPU:0, one launch (start us, length us, event | category | flops | bytes accessed | tf_op | source)
XLA Modules:
  0.0 44.3 jit_solution(7430553738224111)
XLA Ops:
  0.6 40.3 %shard_map.122 = (bf16[128,256]{1,0:T(8,128)(2,1)}, bf16[128,2048]{1,0:T(8,128)(2,1)}) custom-call(bf16[128,2048]{1,0:T(8,128)(2,1)} %hidden_hbm.1, bf16[128,256]{1,0:T(8,128)(2,1)} %fresh_hbm.1, s32[1,128]{1,0:T(1,128)} %bitcast.9, s32[1,128]{1,0:T(1,128)} %bitcast.10, s32[1,128]{1,0:T(1,128)} %bitcast.11, bf16[128,2048]{1,0:T(8,128)(2,1)} %q_hbm.1, ...), custom_call_target="tpu_custom_call" | custom-call | tf_op jit(solution)/shard_map/pallas_call | solution.py:363
  41.0 1.5 %copy.15 = bf16[128,256]{1,0:T(8,128)(2,1)} copy(bf16[128,256]{1,0:T(8,128)(2,1)} %get-tuple-element.4) | data formatting | bytes 131072
  42.4 1.9 %copy.16 = bf16[128,2048]{1,0:T(8,128)(2,1)} copy(bf16[128,2048]{1,0:T(8,128)(2,1)} %get-tuple-element.5) | data formatting | bytes 1048576

commit v3 on v2

--- a/solution.py
+++ b/solution.py
@@ -32,7 +32,7 @@
     hidden, fresh, lengths, index, places,
     q_v, k_v, v_v, w_v, down_v, up_v, local_sem,
     shards, out_rows, in_rows, out_ids, in_ids, slots, part, parts, out_delta, in_delta,
-    mixed_v, own_v, length_v, value_v,
+    mixed_v, own_v, length_v, value_v, value_b, attended_v, store_sem,
     gather_send, gather_recv, row_send, row_recv, id_send, id_recv,
     part_send, part_recv, delta_send, delta_recv,
 ):
@@ -138,7 +138,7 @@
     pl.semaphore_wait(barrier, reps - 1 + tps - 1)
 
     def send_rows(i, c):
-        d = rep_near(reps - 1 - i)
+        d = rep_near(1 + i)
         dispatch = fill(d)
         out_rows[d] = dot(dispatch[:cap], hidden[...]).astype(BF16)
         row_copy(d).start()
@@ -202,27 +202,6 @@
                 own_v[at, h] = own_weight[j]
         return c
 
-    blocks = rows // ROW_BLOCK
-    early = blocks // 2
-    lax.fori_loop(0, early, attend, 0)
-    for k in range(1, half):
-        q = tp_at(2 * k)
-        gather_copy(hidden, q, q, 0).wait_recv()
-        gather_copy(shards.at[q], sibling, q, half + k).start()
-    lax.fori_loop(early, blocks, attend, 0)
-
-    loads[4].wait()
-    base = dot(hidden[...], w_v[me_t])
-    for k in range(1, half):
-        q = tp_at(2 * k)
-        base = base + dot(shards[q], w_v[q])
-    for k in range(half):
-        q = lax.rem(sibling + 2 * k, tps)
-        gather_copy(hidden, q, q, 0).wait_recv()
-        base = base + dot(shards[q], w_v[q])
-
-    loads[3].wait()
-    loads[5].wait()
 
     def part_copy(k, s):
         return pltpu.make_async_remote_copy(
@@ -267,31 +246,45 @@
         spread = jnp.where(chosen(s), total[None], 0.0).reshape(stored * rank, cap).astype(BF16)
         return (ADAPTER_SCALE * dot(spread, up_v[...], TN)).astype(BF16)
 
+    def forward():
+        for k in range(1, half):
+            q = tp_at(2 * k)
+            gather_copy(hidden, q, q, 0).wait_recv()
+            gather_copy(shards.at[q], sibling, q, half + k).start()
+        loads[4].wait()
+        value_v[...] = dot(hidden[...], w_v[me_t])
+        in_delta[me_r] = expand(me_r)
+
+    def finish_base():
+        base = value_v[...]
+        for k in range(1, half):
+            q = tp_at(2 * k)
+            base = base + dot(shards[q], w_v[q])
+        for k in range(half):
+            q = lax.rem(sibling + 2 * k, tps)
+            gather_copy(hidden, q, q, 0).wait_recv()
+            base = base + dot(shards[q], w_v[q])
+        value_v[...] = base + dot(slots[me_r][:cap], in_delta[me_r], TN)
+
     def step(i, c):
         s = rep_near(i)
         row_arrival(s).wait_recv()
         id_arrival(s).wait_recv()
         shrink(s)
-
-        @pl.when(i == 1)
-        def _():
-            in_delta[me_r] = expand(me_r)
-
-        @pl.when(i > 1)
-        def _():
-            back = rep_near(i - 1)
-            out_delta[back] = expand(back)
-            delta_copy(back).start()
-
-        return c
-
+        pl.when(i == 1)(forward)
+        pl.when(i == min(2, reps - 1))(finish_base)
+        out_delta[s] = expand(s)
+        delta_copy(s).start()
+        return c
+
+    blocks = rows // ROW_BLOCK
+    early = blocks // 2
+    lax.fori_loop(0, early, attend, 0)
+    loads[3].wait()
+    loads[5].wait()
     shrink(me_r)
+    lax.fori_loop(early, blocks, attend, 0)
     lax.fori_loop(1, reps, step, 0)
-    last = rep_near(reps - 1)
-    out_delta[last] = expand(last)
-    delta_copy(last).start()
-
-    value_v[...] = base + dot(slots[me_r][:cap], in_delta[me_r], TN)
 
     def collect(i, c):
         s = rep_near(i)
@@ -302,12 +295,19 @@
     lax.fori_loop(1, reps, collect, 0)
 
     value = value_v[...].astype(BF16)
-    value_out[...] = value
+    value_b[...] = value
+    stores = [pltpu.make_async_copy(value_b, value_out, store_sem.at[0])]
+    stores[0].start()
     fresh_value = value.astype(F32)
     for g in range(kv_local):
         for j in range(group):
             h = slice((g * group + j) * HD, (g * group + j + 1) * HD)
-            attended_out[:, h] = (mixed_v[:, h] + own_v[:, h] * fresh_value[:, g * HD:(g + 1) * HD]).astype(BF16)
+            attended_v[:, h] = (mixed_v[:, h] + own_v[:, h] * fresh_value[:, g * HD:(g + 1) * HD]).astype(BF16)
+        part_cols = pl.ds(g * group * HD, group * HD)
+        stores.append(
+            pltpu.make_async_copy(attended_v.at[:, part_cols], attended_out.at[:, part_cols], store_sem.at[1 + g])
+        )
+        stores[-1].start()
 
     gather_copy(hidden, sibling, me_t, 0).wait_send()
     for k in range(1, half):
@@ -329,6 +329,19 @@
         return c
 
     lax.fori_loop(0, reps, drain_parts, 0)
+    for store in stores:
+        store.wait()
+
+
+def hand_over(value, attended, value_out, attended_out, sem):
+    copies = [
+        pltpu.make_async_copy(value, value_out, sem.at[0]),
+        pltpu.make_async_copy(attended, attended_out, sem.at[1]),
+    ]
+    for copy in copies:
+        copy.start()
+    for copy in copies:
+        copy.wait()
 
 
 def shards_fn(
@@ -356,18 +369,17 @@
         vmem((reps, rank, cap), F32), vmem((tps, reps, rank, cap), F32),
         vmem((reps, cap, out_width), BF16), vmem((reps, cap, out_width), BF16),
         vmem(queries.shape, F32), vmem(queries.shape, F32), vmem((rows, HD), F32), vmem((rows, out_width), F32),
+        vmem((rows, out_width), BF16), vmem(queries.shape, BF16), dma((1 + out_width // HD,)),
         dma((tps,)), dma((tps,)), dma((reps,)), dma((reps,)), dma((reps,)), dma((reps,)),
         dma((tps, reps)), dma((tps, reps)), dma((reps,)), dma((reps,)),
     ]
-    vm, anywhere = pl.BlockSpec(memory_space=pltpu.VMEM), pl.BlockSpec(memory_space=pl.ANY)
-    return pl.pallas_call(
+    anywhere = pl.BlockSpec(memory_space=pl.ANY)
+    results = (jax.ShapeDtypeStruct((rows, out_width), BF16), jax.ShapeDtypeStruct(queries.shape, BF16))
+    value, attended = pl.pallas_call(
         functools.partial(kernel, reps, tps, cap, stored, rank),
-        out_shape=(
-            jax.ShapeDtypeStruct((rows, out_width), BF16),
-            jax.ShapeDtypeStruct(queries.shape, BF16),
-        ),
+        out_shape=results,
         in_specs=[anywhere] * 11,
-        out_specs=(vm, vm),
+        out_specs=(anywhere, anywhere),
         scratch_shapes=scratch,
         compiler_params=pltpu.CompilerParams(
             collective_id=0, has_side_effects=True, vmem_limit_bytes=60 * 1024 * 1024
@@ -377,6 +389,14 @@
         adapter_table_place.reshape(1, -1), queries, cached_key_rows, cached_value_rows, w,
         adapter_down_factor.reshape(stored * rank, width), adapter_up_factor.reshape(stored * rank, out_width),
     )
+    return pl.pallas_call(
+        hand_over,
+        out_shape=results,
+        in_specs=[anywhere] * 2,
+        out_specs=(anywhere, anywhere),
+        scratch_shapes=[dma((2,))],
+        compiler_params=pltpu.CompilerParams(vmem_limit_bytes=60 * 1024 * 1024),
+    )(value, attended)
 
 
 def solution(mesh):

time: 44.5 us -> 57.8 us (1.30)
  Pallas kernels: 40.3 us -> 57 us
  local copies, waits for them, and re-layouts: 3.35 us -> 0 us
    pallas_call x0 -> x1, Pallas kernels: none -> 19 us  [shards_fn(): pl.pallas_call(hand_over, out_shape=results, in_specs=[anywhere] * 2, out...]
    unnamed x2 -> x0, local copies, waits for them, and re-layouts: 3.35 us -> none
    pallas_call x1, Pallas kernels: 40.3 us -> 38 us  [shards_fn(): pl.pallas_call(functools.partial(kernel, reps, tps, cap, stored, rank), o...]
where the time goes in v3:
time: 57.8 us; the launch traced here: 57.6 us
  Pallas kernels  57 us (99%)
  between operations  0.64 us (1%)
    pallas_call x1, Pallas kernels, shards_fn(): pl.pallas_call(functools.partial(kernel, reps, tps, cap, stored, rank), o...  38 us
    pallas_call x1, Pallas kernels, shards_fn(): pl.pallas_call(hand_over, out_shape=results, in_specs=[anywhere] * 2, out...  19 us

profile of v3, /device:TPU:0, one launch (start us, length us, event | category | flops | bytes accessed | tf_op | source)
XLA Modules:
  0.0 57.6 jit_solution(9435868633604524197)
XLA Ops:
  0.6 38.0 %shard_map.122 = (bf16[128,256]{1,0:T(8,128)(2,1)}, bf16[128,2048]{1,0:T(8,128)(2,1)}) custom-call(bf16[128,2048]{1,0:T(8,128)(2,1)} %hidden_hbm.1, bf16[128,256]{1,0:T(8,128)(2,1)} %fresh_hbm.1, s32[1,128]{1,0:T(1,128)} %bitcast.9, s32[1,128]{1,0:T(1,128)} %bitcast.10, s32[1,128]{1,0:T(1,128)} %bitcast.11, bf16[128,2048]{1,0:T(8,128)(2,1)} %q_hbm.1, ...), custom_call_target="tpu_custom_call" | custom-call | tf_op jit(solution)/shard_map/pallas_call | solution.py:378
  38.6 19.0 %shard_map.123 = (bf16[128,256]{1,0:T(8,128)(2,1)}, bf16[128,2048]{1,0:T(8,128)(2,1)}) custom-call(bf16[128,256]{1,0:T(8,128)(2,1)} %get-tuple-element.4.value, bf16[128,2048]{1,0:T(8,128)(2,1)} %get-tuple-element.5.attended), custom_call_target="tpu_custom_call" | custom-call | tf_op jit(solution)/shard_map/pallas_call | solution.py:392

commit v4 on v3

--- a/solution.py
+++ b/solution.py
@@ -28,11 +28,11 @@
 def kernel(
     reps, tps, cap, stored, rank,
     hidden_hbm, fresh_hbm, lengths_hbm, index_hbm, places_hbm, q_hbm, k_hbm, v_hbm, w_hbm, down_hbm, up_hbm,
-    value_out, attended_out,
+    value_out, mixed_out, own_out,
     hidden, fresh, lengths, index, places,
     q_v, k_v, v_v, w_v, down_v, up_v, local_sem,
     shards, out_rows, in_rows, out_ids, in_ids, slots, part, parts, out_delta, in_delta,
-    mixed_v, own_v, length_v, value_v, value_b, attended_v, store_sem,
+    mixed_v, own_v, length_v, value_v, value_b, store_sem,
     gather_send, gather_recv, row_send, row_recv, id_send, id_recv,
     part_send, part_recv, delta_send, delta_recv,
 ):
@@ -174,6 +174,8 @@
         low = (iota((ROW_BLOCK, span), 0) * positions).astype(F32)
         high = low + length_v[at, 0:1]
         bias = jnp.where((column >= low) & (column < high), 0.0, MASKED)
+        lane = iota((ROW_BLOCK, HD), 1)
+        own_lanes = jnp.zeros((ROW_BLOCK, HD), F32)
         for g in range(kv_local):
             feats = slice(g * HD, (g + 1) * HD)
             heads = [slice((g * group + j) * HD, (g * group + j + 1) * HD) for j in range(group)]
@@ -193,13 +195,12 @@
             own_expo = jnp.exp(own - top)
             scale = 1.0 / (jnp.sum(expo, axis=-1, keepdims=True) + own_expo)
             weights = (expo * scale).astype(BF16).reshape(group * ROW_BLOCK, span)
-            own_weight = jnp.broadcast_to(
-                (own_expo * scale).astype(BF16).astype(F32), (group, ROW_BLOCK, HD)
-            )
+            own_weight = (own_expo * scale).astype(BF16).astype(F32)
             mixed = dot(weights, values)
             for j, h in enumerate(heads):
                 mixed_v[at, h] = mixed[j * ROW_BLOCK:(j + 1) * ROW_BLOCK]
-                own_v[at, h] = own_weight[j]
+                own_lanes = jnp.where(lane == g * group + j, own_weight[j], own_lanes)
+        own_v[at, :] = own_lanes
         return c
 
 
@@ -284,6 +285,10 @@
     loads[5].wait()
     shrink(me_r)
     lax.fori_loop(early, blocks, attend, 0)
+    store_mixed = pltpu.make_async_copy(mixed_v, mixed_out, store_sem.at[1])
+    store_own = pltpu.make_async_copy(own_v, own_out, store_sem.at[2])
+    store_mixed.start()
+    store_own.start()
     lax.fori_loop(1, reps, step, 0)
 
     def collect(i, c):
@@ -296,18 +301,8 @@
 
     value = value_v[...].astype(BF16)
     value_b[...] = value
-    stores = [pltpu.make_async_copy(value_b, value_out, store_sem.at[0])]
-    stores[0].start()
-    fresh_value = value.astype(F32)
-    for g in range(kv_local):
-        for j in range(group):
-            h = slice((g * group + j) * HD, (g * group + j + 1) * HD)
-            attended_v[:, h] = (mixed_v[:, h] + own_v[:, h] * fresh_value[:, g * HD:(g + 1) * HD]).astype(BF16)
-        part_cols = pl.ds(g * group * HD, group * HD)
-        stores.append(
-            pltpu.make_async_copy(attended_v.at[:, part_cols], attended_out.at[:, part_cols], store_sem.at[1 + g])
-        )
-        stores[-1].start()
+    store_value = pltpu.make_async_copy(value_b, value_out, store_sem.at[0])
+    store_value.start()
 
     gather_copy(hidden, sibling, me_t, 0).wait_send()
     for k in range(1, half):
@@ -329,19 +324,33 @@
         return c
 
     lax.fori_loop(0, reps, drain_parts, 0)
+    for store in (store_value, store_mixed, store_own):
+        store.wait()
+
+
+def combine(value_hbm, mixed_hbm, own_hbm, value_out, attended_out, value_v, mixed_v, own_v, attended_v, sem):
+    kv_local = value_v.shape[1] // HD
+    width = mixed_v.shape[1] // kv_local
+    parts = [slice(g * width, (g + 1) * width) for g in range(kv_local)]
+    loads = [pltpu.make_async_copy(value_hbm, value_v, sem.at[0]), pltpu.make_async_copy(own_hbm, own_v, sem.at[1])]
+    loads += [pltpu.make_async_copy(mixed_hbm.at[:, p], mixed_v.at[:, p], sem.at[2 + g]) for g, p in enumerate(parts)]
+    for load in loads:
+        load.start()
+    loads[0].wait()
+    stores = [pltpu.make_async_copy(value_v, value_out, sem.at[2 + kv_local])]
+    stores[0].start()
+    loads[1].wait()
+    for g, p in enumerate(parts):
+        loads[2 + g].wait()
+        value = value_v[:, g * HD:(g + 1) * HD].astype(F32)
+        for j in range(width // HD):
+            n = g * (width // HD) + j
+            h = slice(n * HD, (n + 1) * HD)
+            attended_v[:, h] = (mixed_v[:, h] + own_v[:, n:n + 1] * value).astype(BF16)
+        stores.append(pltpu.make_async_copy(attended_v.at[:, p], attended_out.at[:, p], sem.at[3 + kv_local + g]))
+        stores[-1].start()
     for store in stores:
         store.wait()
-
-
-def hand_over(value, attended, value_out, attended_out, sem):
-    copies = [
-        pltpu.make_async_copy(value, value_out, sem.at[0]),
-        pltpu.make_async_copy(attended, attended_out, sem.at[1]),
-    ]
-    for copy in copies:
-        copy.start()
-    for copy in copies:
-        copy.wait()
 
 
 def shards_fn(
@@ -368,18 +377,20 @@
         vmem((reps, rows, rows), BF16),
         vmem((reps, rank, cap), F32), vmem((tps, reps, rank, cap), F32),
         vmem((reps, cap, out_width), BF16), vmem((reps, cap, out_width), BF16),
-        vmem(queries.shape, F32), vmem(queries.shape, F32), vmem((rows, HD), F32), vmem((rows, out_width), F32),
-        vmem((rows, out_width), BF16), vmem(queries.shape, BF16), dma((1 + out_width // HD,)),
+        vmem(queries.shape, F32), vmem((rows, HD), F32), vmem((rows, HD), F32), vmem((rows, out_width), F32),
+        vmem((rows, out_width), BF16), dma((3,)),
         dma((tps,)), dma((tps,)), dma((reps,)), dma((reps,)), dma((reps,)), dma((reps,)),
         dma((tps, reps)), dma((tps, reps)), dma((reps,)), dma((reps,)),
     ]
     anywhere = pl.BlockSpec(memory_space=pl.ANY)
     results = (jax.ShapeDtypeStruct((rows, out_width), BF16), jax.ShapeDtypeStruct(queries.shape, BF16))
-    value, attended = pl.pallas_call(
+    value, mixed, own = pl.pallas_call(
         functools.partial(kernel, reps, tps, cap, stored, rank),
-        out_shape=results,
+        out_shape=(
+            results[0], jax.ShapeDtypeStruct(queries.shape, F32), jax.ShapeDtypeStruct((rows, HD), F32),
+        ),
         in_specs=[anywhere] * 11,
-        out_specs=(anywhere, anywhere),
+        out_specs=(anywhere,) * 3,
         scratch_shapes=scratch,
         compiler_params=pltpu.CompilerParams(
             collective_id=0, has_side_effects=True, vmem_limit_bytes=60 * 1024 * 1024
@@ -390,13 +401,16 @@
         adapter_down_factor.reshape(stored * rank, width), adapter_up_factor.reshape(stored * rank, out_width),
     )
     return pl.pallas_call(
-        hand_over,
+        combine,
         out_shape=results,
-        in_specs=[anywhere] * 2,
+        in_specs=[anywhere] * 3,
         out_specs=(anywhere, anywhere),
-        scratch_shapes=[dma((2,))],
+        scratch_shapes=[
+            vmem((rows, out_width), BF16), vmem(queries.shape, F32), vmem((rows, HD), F32), vmem(queries.shape, BF16),
+            dma((3 + 2 * (out_width // HD),)),
+        ],
         compiler_params=pltpu.CompilerParams(vmem_limit_bytes=60 * 1024 * 1024),
-    )(value, attended)
+    )(value, mixed, own)
 
 
 def solution(mesh):

time: 57.8 us -> 40.9 us (0.71)
  Pallas kernels: 57 us -> 40.1 us
    pallas_call x1, Pallas kernels: 19 us -> 2.31 us  [shards_fn(): pl.pallas_call(combine, out_shape=results, in_specs=[anywhere] * 3, out_s...]
where the time goes in v4:
time: 40.9 us; the launch traced here: 40.7 us
  Pallas kernels  40.1 us (98%)
  between operations  0.64 us (2%)
    pallas_call x1, Pallas kernels, shards_fn(): pl.pallas_call(functools.partial(kernel, reps, tps, cap, stored, rank), o...  37.8 us
    pallas_call x1, Pallas kernels, shards_fn(): pl.pallas_call(combine, out_shape=results, in_specs=[anywhere] * 3, out_s...  2.31 us

profile of v4, /device:TPU:0, one launch (start us, length us, event | category | flops | bytes accessed | tf_op | source)
XLA Modules:
  0.0 40.7 jit_solution(11835648746756172766)
XLA Ops:
  0.6 37.8 %shard_map.122 = (bf16[128,256]{1,0:T(8,128)(2,1)}, f32[128,2048]{1,0:T(8,128)}, f32[128,128]{1,0:T(8,128)}) custom-call(bf16[128,2048]{1,0:T(8,128)(2,1)} %hidden_hbm.1, bf16[128,256]{1,0:T(8,128)(2,1)} %fresh_hbm.1, s32[1,128]{1,0:T(1,128)} %bitcast.9, s32[1,128]{1,0:T(1,128)} %bitcast.10, s32[1,128]{1,0:T(1,128)} %bitcast.11, bf16[128,2048]{1,0:T(8,128)(2,1)} %q_hbm.1, ...), custom_call_target="tpu_custom_call" | custom-call | tf_op jit(solution)/shard_map/pallas_call | solution.py:387
  38.4 2.3 %shard_map.123 = (bf16[128,256]{1,0:T(8,128)(2,1)}, bf16[128,2048]{1,0:T(8,128)(2,1)}) custom-call(bf16[128,256]{1,0:T(8,128)(2,1)} %get-tuple-element.5.value_hbm, f32[128,2048]{1,0:T(8,128)} %get-tuple-element.6.mixed_hbm, f32[128,128]{1,0:T(8,128)} %get-tuple-element.7.own_hbm), custom_call_target="tpu_custom_call" | custom-call | tf_op jit(solution)/shard_map/pallas_call | solution.py:403

commit v5 on v4

--- a/solution.py
+++ b/solution.py
@@ -28,11 +28,11 @@
 def kernel(
     reps, tps, cap, stored, rank,
     hidden_hbm, fresh_hbm, lengths_hbm, index_hbm, places_hbm, q_hbm, k_hbm, v_hbm, w_hbm, down_hbm, up_hbm,
-    value_out, mixed_out, own_out,
+    value_b, mixed_v, own_v,
     hidden, fresh, lengths, index, places,
     q_v, k_v, v_v, w_v, down_v, up_v, local_sem,
     shards, out_rows, in_rows, out_ids, in_ids, slots, part, parts, out_delta, in_delta,
-    mixed_v, own_v, length_v, value_v, value_b, store_sem,
+    length_v, value_v,
     gather_send, gather_recv, row_send, row_recv, id_send, id_recv,
     part_send, part_recv, delta_send, delta_recv,
 ):
@@ -65,7 +65,7 @@
             )
         )
     ]
-    for n in (6, 7, 8, 9, 10, 0, 1, 2, 3, 5, 4):
+    for n in (6, 7, 8):
         loads[n].start()
 
     barrier = pltpu.get_barrier_semaphore()
@@ -135,13 +135,17 @@
         return dispatch
 
     loads[8].wait()
+    for n in (9, 10, 0, 1, 2, 3, 5, 4):
+        loads[n].start()
     pl.semaphore_wait(barrier, reps - 1 + tps - 1)
+
+    direct = reps // 2
 
     def send_rows(i, c):
         d = rep_near(1 + i)
         dispatch = fill(d)
         out_rows[d] = dot(dispatch[:cap], hidden[...]).astype(BF16)
-        row_copy(d).start()
+        pl.when(i < direct)(row_copy(d).start)
         out_ids[d] = dot(inner, dispatch, NT)
         id_copy(d).start()
         return c
@@ -285,10 +289,13 @@
     loads[5].wait()
     shrink(me_r)
     lax.fori_loop(early, blocks, attend, 0)
-    store_mixed = pltpu.make_async_copy(mixed_v, mixed_out, store_sem.at[1])
-    store_own = pltpu.make_async_copy(own_v, own_out, store_sem.at[2])
-    store_mixed.start()
-    store_own.start()
+
+    def send_later(i, c):
+        row_copy(rep_near(1 + i - 1)).wait_send()
+        row_copy(rep_near(1 + i)).start()
+        return c
+
+    lax.fori_loop(direct, reps - 1, send_later, 0)
     lax.fori_loop(1, reps, step, 0)
 
     def collect(i, c):
@@ -299,10 +306,7 @@
 
     lax.fori_loop(1, reps, collect, 0)
 
-    value = value_v[...].astype(BF16)
-    value_b[...] = value
-    store_value = pltpu.make_async_copy(value_b, value_out, store_sem.at[0])
-    store_value.start()
+    value_b[...] = value_v[...].astype(BF16)
 
     gather_copy(hidden, sibling, me_t, 0).wait_send()
     for k in range(1, half):
@@ -310,8 +314,8 @@
         gather_copy(hidden, sibling, me_t, half + k).wait_send()
 
     def drain(i, c):
-        d = rep_at(i)
-        row_copy(d).wait_send()
+        d = rep_near(i)
+        pl.when((i < direct) | (i == reps - 1))(row_copy(d).wait_send)
         id_copy(d).wait_send()
         delta_copy(d).wait_send()
         return c
@@ -324,30 +328,21 @@
         return c
 
     lax.fori_loop(0, reps, drain_parts, 0)
-    for store in (store_value, store_mixed, store_own):
-        store.wait()
-
-
-def combine(value_hbm, mixed_hbm, own_hbm, value_out, attended_out, value_v, mixed_v, own_v, attended_v, sem):
+
+
+def combine(value_v, mixed_v, own_v, value_out, attended_out, attended_v, sem):
     kv_local = value_v.shape[1] // HD
     width = mixed_v.shape[1] // kv_local
-    parts = [slice(g * width, (g + 1) * width) for g in range(kv_local)]
-    loads = [pltpu.make_async_copy(value_hbm, value_v, sem.at[0]), pltpu.make_async_copy(own_hbm, own_v, sem.at[1])]
-    loads += [pltpu.make_async_copy(mixed_hbm.at[:, p], mixed_v.at[:, p], sem.at[2 + g]) for g, p in enumerate(parts)]
-    for load in loads:
-        load.start()
-    loads[0].wait()
-    stores = [pltpu.make_async_copy(value_v, value_out, sem.at[2 + kv_local])]
+    stores = [pltpu.make_async_copy(value_v, value_out, sem.at[0])]
     stores[0].start()
-    loads[1].wait()
-    for g, p in enumerate(parts):
-        loads[2 + g].wait()
+    for g in range(kv_local):
         value = value_v[:, g * HD:(g + 1) * HD].astype(F32)
         for j in range(width // HD):
             n = g * (width // HD) + j
             h = slice(n * HD, (n + 1) * HD)
             attended_v[:, h] = (mixed_v[:, h] + own_v[:, n:n + 1] * value).astype(BF16)
-        stores.append(pltpu.make_async_copy(attended_v.at[:, p], attended_out.at[:, p], sem.at[3 + kv_local + g]))
+        p = slice(g * width, (g + 1) * width)
+        stores.append(pltpu.make_async_copy(attended_v.at[:, p], attended_out.at[:, p], sem.at[1 + g]))
         stores[-1].start()
     for store in stores:
         store.wait()
@@ -377,20 +372,19 @@
         vmem((reps, rows, rows), BF16),
         vmem((reps, rank, cap), F32), vmem((tps, reps, rank, cap), F32),
         vmem((reps, cap, out_width), BF16), vmem((reps, cap, out_width), BF16),
-        vmem(queries.shape, F32), vmem((rows, HD), F32), vmem((rows, HD), F32), vmem((rows, out_width), F32),
-        vmem((rows, out_width), BF16), dma((3,)),
+        vmem((rows, HD), F32), vmem((rows, out_width), F32),
         dma((tps,)), dma((tps,)), dma((reps,)), dma((reps,)), dma((reps,)), dma((reps,)),
         dma((tps, reps)), dma((tps, reps)), dma((reps,)), dma((reps,)),
     ]
-    anywhere = pl.BlockSpec(memory_space=pl.ANY)
+    anywhere, inside = pl.BlockSpec(memory_space=pl.ANY), pl.BlockSpec(memory_space=pltpu.VMEM)
     results = (jax.ShapeDtypeStruct((rows, out_width), BF16), jax.ShapeDtypeStruct(queries.shape, BF16))
     value, mixed, own = pl.pallas_call(
         functools.partial(kernel, reps, tps, cap, stored, rank),
         out_shape=(
-            results[0], jax.ShapeDtypeStruct(queries.shape, F32), jax.ShapeDtypeStruct((rows, HD), F32),
+            vmem((rows, out_width), BF16), vmem(queries.shape, F32), vmem((rows, HD), F32),
         ),
         in_specs=[anywhere] * 11,
-        out_specs=(anywhere,) * 3,
+        out_specs=(inside,) * 3,
         scratch_shapes=scratch,
         compiler_params=pltpu.CompilerParams(
             collective_id=0, has_side_effects=True, vmem_limit_bytes=60 * 1024 * 1024
@@ -403,13 +397,10 @@
     return pl.pallas_call(
         combine,
         out_shape=results,
-        in_specs=[anywhere] * 3,
+        in_specs=[inside] * 3,
         out_specs=(anywhere, anywhere),
-        scratch_shapes=[
-            vmem((rows, out_width), BF16), vmem(queries.shape, F32), vmem((rows, HD), F32), vmem(queries.shape, BF16),
-            dma((3 + 2 * (out_width // HD),)),
-        ],
-        compiler_params=pltpu.CompilerParams(vmem_limit_bytes=60 * 1024 * 1024),
+        scratch_shapes=[vmem(queries.shape, BF16), dma((1 + out_width // HD,))],
+        compiler_params=pltpu.CompilerParams(vmem_limit_bytes=16 * 1024 * 1024),
     )(value, mixed, own)
 
 

time: 40.9 us -> 38.5 us (0.941)
  the two profiles are of different devices: /device:TPU:0 before, /device:TPU:8 now
where the time goes in v5:
time: 38.5 us; the launch traced here: 38.3 us
  Pallas kernels  37.7 us (98%)
  between operations  0.64 us (2%)
    pallas_call x1, Pallas kernels, shards_fn(): pl.pallas_call(functools.partial(kernel, reps, tps, cap, stored, rank), o...  36.6 us
    pallas_call x1, Pallas kernels, shards_fn(): pl.pallas_call(combine, out_shape=results, in_specs=[inside] * 3, out_spe...  1.09 us

profile of v5, /device:TPU:8, one launch (start us, length us, event | category | flops | bytes accessed | tf_op | source)
XLA Modules:
  0.0 38.3 jit_solution(8874101954328054172)
XLA Ops:
  0.6 36.6 %shard_map.122 = (bf16[128,256]{1,0:T(8,128)(2,1)S(1)}, f32[128,2048]{1,0:T(8,128)S(1)}, f32[128,128]{1,0:T(8,128)S(1)}) custom-call(bf16[128,2048]{1,0:T(8,128)(2,1)} %hidden_hbm.1, bf16[128,256]{1,0:T(8,128)(2,1)} %fresh_hbm.1, s32[1,128]{1,0:T(1,128)} %bitcast.9, s32[1,128]{1,0:T(1,128)} %bitcast.10, s32[1,128]{1,0:T(1,128)} %bitcast.11, ...), custom_call_target="tpu_custom_call" | custom-call | tf_op jit(solution)/shard_map/pallas_call | solution.py:381
  37.2 1.1 %shard_map.123 = (bf16[128,256]{1,0:T(8,128)(2,1)}, bf16[128,2048]{1,0:T(8,128)(2,1)}) custom-call(bf16[128,256]{1,0:T(8,128)(2,1)S(1)} %get-tuple-element.5.value_v, f32[128,2048]{1,0:T(8,128)S(1)} %get-tuple-element.6.mixed_v, f32[128,128]{1,0:T(8,128)S(1)} %get-tuple-element.7.own_v), custom_call_target="tpu_custom_call" | custom-call | tf_op jit(solution)/shard_map/pallas_call | solution.py:397

commit v6 on v5

--- a/solution.py
+++ b/solution.py
@@ -142,7 +142,7 @@
     direct = reps // 2
 
     def send_rows(i, c):
-        d = rep_near(1 + i)
+        d = rep_near(jnp.where(i < direct, direct - i, 1 + i))
         dispatch = fill(d)
         out_rows[d] = dot(dispatch[:cap], hidden[...]).astype(BF16)
         pl.when(i < direct)(row_copy(d).start)
@@ -291,7 +291,7 @@
     lax.fori_loop(early, blocks, attend, 0)
 
     def send_later(i, c):
-        row_copy(rep_near(1 + i - 1)).wait_send()
+        row_copy(rep_near(i)).wait_send()
         row_copy(rep_near(1 + i)).start()
         return c
 

time: 38.5 us -> 38 us (0.987)
  Pallas kernels: 37.7 us -> 37.2 us
    pallas_call x1, Pallas kernels: 36.6 us -> 36.1 us  [shards_fn(): pl.pallas_call(functools.partial(kernel, reps, tps, cap, stored, rank), o...]
where the time goes in v6:
time: 38 us; the launch traced here: 37.8 us
  Pallas kernels  37.2 us (98%)
  between operations  0.64 us (2%)
    pallas_call x1, Pallas kernels, shards_fn(): pl.pallas_call(functools.partial(kernel, reps, tps, cap, stored, rank), o...  36.1 us
    pallas_call x1, Pallas kernels, shards_fn(): pl.pallas_call(combine, out_shape=results, in_specs=[inside] * 3, out_spe...  1.09 us

profile of v6, /device:TPU:8, one launch (start us, length us, event | category | flops | bytes accessed | tf_op | source)
XLA Modules:
  0.0 37.8 jit_solution(7358808932346345511)
XLA Ops:
  0.6 36.1 %shard_map.122 = (bf16[128,256]{1,0:T(8,128)(2,1)S(1)}, f32[128,2048]{1,0:T(8,128)S(1)}, f32[128,128]{1,0:T(8,128)S(1)}) custom-call(bf16[128,2048]{1,0:T(8,128)(2,1)} %hidden_hbm.1, bf16[128,256]{1,0:T(8,128)(2,1)} %fresh_hbm.1, s32[1,128]{1,0:T(1,128)} %bitcast.9, s32[1,128]{1,0:T(1,128)} %bitcast.10, s32[1,128]{1,0:T(1,128)} %bitcast.11, ...), custom_call_target="tpu_custom_call" | custom-call | tf_op jit(solution)/shard_map/pallas_call | solution.py:381
  36.7 1.1 %shard_map.123 = (bf16[128,256]{1,0:T(8,128)(2,1)}, bf16[128,2048]{1,0:T(8,128)(2,1)}) custom-call(bf16[128,256]{1,0:T(8,128)(2,1)S(1)} %get-tuple-element.5.value_v, f32[128,2048]{1,0:T(8,128)S(1)} %get-tuple-element.6.mixed_v, f32[128,128]{1,0:T(8,128)S(1)} %get-tuple-element.7.own_v), custom_call_target="tpu_custom_call" | custom-call | tf_op jit(solution)/shard_map/pallas_call | solution.py:397

commit v7 on v6

--- a/solution.py
+++ b/solution.py
@@ -239,7 +239,7 @@
     def shrink(s):
         full = dot(down_v[...], in_rows[s], NT).reshape(stored, rank, cap)
         part[s] = jnp.sum(jnp.where(chosen(s), full, 0.0), axis=0)
-        for k in range(1, tps):
+        for k in range(tps - 1, 0, -1):
             part_copy(k, s).start()
 
     def expand(s):
@@ -271,6 +271,11 @@
             base = base + dot(shards[q], w_v[q])
         value_v[...] = base + dot(slots[me_r][:cap], in_delta[me_r], TN)
 
+    def turn(i, c):
+        s = rep_near(i)
+        slots[s] = jnp.transpose(slots[s].astype(F32)).astype(BF16)
+        return c
+
     def step(i, c):
         s = rep_near(i)
         row_arrival(s).wait_recv()
@@ -278,6 +283,7 @@
         shrink(s)
         pl.when(i == 1)(forward)
         pl.when(i == min(2, reps - 1))(finish_base)
+        turn(i, c)
         out_delta[s] = expand(s)
         delta_copy(s).start()
         return c
@@ -301,7 +307,7 @@
     def collect(i, c):
         s = rep_near(i)
         delta_arrival(s).wait_recv()
-        value_v[...] += dot(slots[s][:cap], in_delta[s], TN)
+        value_v[...] += dot(slots[s][:, :cap], in_delta[s])
         return c
 
     lax.fori_loop(1, reps, collect, 0)

time: 38 us -> 38 us (level)
  no operation moved by 1% of the time
where the time goes in v7:
time: 38 us; the launch traced here: 37.8 us
  Pallas kernels  37.2 us (98%)
  between operations  0.64 us (2%)
    pallas_call x1, Pallas kernels, shards_fn(): pl.pallas_call(functools.partial(kernel, reps, tps, cap, stored, rank), o...  36.1 us
    pallas_call x1, Pallas kernels, shards_fn(): pl.pallas_call(combine, out_shape=results, in_specs=[inside] * 3, out_spe...  1.09 us

profile of v7, /device:TPU:8, one launch (start us, length us, event | category | flops | bytes accessed | tf_op | source)
XLA Modules:
  0.0 37.8 jit_solution(7924662330830012512)
XLA Ops:
  0.6 36.1 %shard_map.122 = (bf16[128,256]{1,0:T(8,128)(2,1)S(1)}, f32[128,2048]{1,0:T(8,128)S(1)}, f32[128,128]{1,0:T(8,128)S(1)}) custom-call(bf16[128,2048]{1,0:T(8,128)(2,1)} %hidden_hbm.1, bf16[128,256]{1,0:T(8,128)(2,1)} %fresh_hbm.1, s32[1,128]{1,0:T(1,128)} %bitcast.9, s32[1,128]{1,0:T(1,128)} %bitcast.10, s32[1,128]{1,0:T(1,128)} %bitcast.11, ...), custom_call_target="tpu_custom_call" | custom-call | tf_op jit(solution)/shard_map/pallas_call | solution.py:387
  36.8 1.1 %shard_map.123 = (bf16[128,256]{1,0:T(8,128)(2,1)}, bf16[128,2048]{1,0:T(8,128)(2,1)}) custom-call(bf16[128,256]{1,0:T(8,128)(2,1)S(1)} %get-tuple-element.5.value_v, f32[128,2048]{1,0:T(8,128)S(1)} %get-tuple-element.6.mixed_v, f32[128,128]{1,0:T(8,128)S(1)} %get-tuple-element.7.own_v), custom_call_target="tpu_custom_call" | custom-call | tf_op jit(solution)/shard_map/pallas_call | solution.py:403
